TPU v7x, 256 devices: a whole 4x4x8 slice. The times are simulated.
256 devices in a mesh: dp: 64 (over z_hi, x, y, core), mp: 4 (over z_lo).
Axes of the slice: x: 4, y: 4, z: 8 (z_hi: 2, z_lo: 4; z = z_hi * 4 + z_lo), core: 2. Of those that a mesh axis runs over, the one named last changes fastest.
Arguments:
- tokens: bfloat16 [8192, 3072], P('dp', 'mp'), may hold values from -16 to 16
- weight: bfloat16 [3072, 12288], P('dp', 'mp'), may hold values from -0.109375 to 0.109375
- logits: float32 [6, 768, 12288], P(None, 'dp', 'mp'), may hold values from -8 to 320
- gumbel: bfloat16 [6, 768, 12288], P(None, 'dp', 'mp'), may hold values from -2 to 7, as said below
- cotangent: bfloat16 [8192, 12288], P('dp', 'mp'), may hold values from -6 to 6
- moment_one: float32 [6, 768, 12288], P(None, 'dp', 'mp'), may hold values from -6 to 6
- moment_two: float32 [6, 768, 12288], P(None, 'dp', 'mp'), may hold values from 0.01 to 1
Outputs:
- output: bfloat16 [8192, 12288], P('dp', 'mp')
- input_grad: bfloat16 [8192, 3072], P('dp', 'mp')
- new_logits: float32 [6, 768, 12288], P(None, 'dp', 'mp')
- new_moment_one: float32 [6, 768, 12288], P(None, 'dp', 'mp')
- new_moment_two: float32 [6, 768, 12288], P(None, 'dp', 'mp')
Inputs may be any that keep to these rules, and one draw needn't show every extreme that they name: `gumbel`: Gumbel(0, 1) noise.
All inputs are finite; a program needn't handle non-finite values.
Results may differ from a plain program's by a relative error of at most 0.002.
The roundings to bfloat16 on the way count: a program that leaves them out, or rounds other values in their place, can miss the bound.
Values may be sent and summed in bfloat16 or wider, within the bound.
No kernel may reach another device: no remote copies, remote signals or barrier semaphores. Data moves between devices by JAX's collectives and lax.ppermute only.
A program may use at most 128 MiB of HBM per device.

v0:
```python
import functools

import jax
import jax.numpy as jnp
import numpy as np
from jax import lax
from jax.experimental import pallas as pl
from jax.experimental.pallas import tpu as pltpu
from jax.sharding import PartitionSpec as P

beta_one = 0.9
beta_two = 0.999
adam_eps = 1e-08
decay = 0.01
rate = 0.1
adam_step = 10.0

F32 = jnp.float32
BF16 = jnp.bfloat16
AXES = ("dp", "mp")
SIZES = (2, 4, 4, 2, 4)
PAIRS = tuple((i, j) for i in range(4) for j in range(i + 1, 4))
ROWS = 48
HALF = 1536
WIDE = 512
TILE = 512
MIB = 1 << 20
IN_VMEM = pl.BlockSpec(memory_space=pltpu.VMEM)
HEAVY = pl.CostEstimate(flops=20000000000, bytes_accessed=1, transcendentals=0)
LIGHT = pl.CostEstimate(flops=0, bytes_accessed=1, transcendentals=0)


def pairs_of(target):
    found = []
    for here in np.ndindex(*SIZES):
        there = tuple(a % b for a, b in zip(target(*here), SIZES))
        found.append(
            (int(np.ravel_multi_index(here, SIZES)), int(np.ravel_multi_index(there, SIZES)))
        )
    return found


def step_a(by):
    return pairs_of(
        lambda z, x, y, c, m: (z, x + by, y, c, m) if c == 0 else (z, x, y + by, c, m)
    )


def step_b(by):
    return pairs_of(
        lambda z, x, y, c, m: (z, x, y + by, c, m) if c == 0 else (z, x + by, y, c, m)
    )


SIBLING = pairs_of(lambda z, x, y, c, m: (z, x, y, c + 1, m))
PARTNER = pairs_of(lambda z, x, y, c, m: (z + 1, x, y, c, m))
A_UP, A_DOWN, A_TWO = step_a(1), step_a(-1), step_a(2)
B_UP, B_DOWN = step_b(1), step_b(-1)


def around(by):
    return pairs_of(lambda z, x, y, c, m: (z, x, y, c, m + by))


def crossed(by):
    return pairs_of(lambda z, x, y, c, m: (z, x, y, c, m ^ by))


def send(value, pairs):
    return lax.ppermute(value, AXES, pairs)


def dot(a, b, dims):
    return lax.dot_general(a, b, (dims, ((), ())), preferred_element_type=F32)


def mask_kernel(logits, gumbel, weight, probs, masked, spread):
    scores = [logits[p] + gumbel[p].astype(F32) for p in range(6)]
    top = scores[0]
    for p in range(1, 6):
        top = jnp.maximum(top, scores[p])
    exps = [jnp.exp(s - top) for s in scores]
    total = exps[0]
    for p in range(1, 6):
        total = total + exps[p]
    share = [e / total for e in exps]
    for p in range(6):
        probs[p] = share[p]
    for slot in range(4):
        kept = [share[p] for p in range(6) if slot in PAIRS[p]]
        mask = kept[0] + kept[1] + kept[2]
        for j in range(WIDE // 128):
            at = j * 128
            spread[pl.ds(j * ROWS + slot, 12, stride=4), :] = mask[:, at : at + 128]
    for j in range(WIDE // 128):
        at = j * 128
        part = weight[:, at : at + 128].astype(F32) * spread[j * ROWS : (j + 1) * ROWS, :]
        masked[:, at : at + 128] = part.astype(BF16)


def make_masked(logits, gumbel, weight):
    cols = weight.shape[1]
    wide = WIDE
    three = pl.BlockSpec((6, 12, wide), lambda i: (0, 0, i))
    two = pl.BlockSpec((ROWS, wide), lambda i: (0, i))
    return pl.pallas_call(
        mask_kernel,
        grid=(cols // wide,),
        in_specs=[three, three, two],
        out_specs=[three, two],
        out_shape=[
            jax.ShapeDtypeStruct((6, 12, cols), F32),
            jax.ShapeDtypeStruct((ROWS, cols), BF16),
        ],
        scratch_shapes=[pltpu.VMEM((wide // 128 * ROWS, 128), F32)],
        compiler_params=pltpu.CompilerParams(vmem_limit_bytes=16 * MIB),
        cost_estimate=LIGHT,
    )(logits, gumbel, weight)


def adam_kernel(wgrad, weight, probs, logits, one, two, new_logits, new_one, new_two, spread):
    for j in range(WIDE // 128):
        at = j * 128
        spread[j * ROWS : (j + 1) * ROWS, :] = (
            weight[:, at : at + 128].astype(F32) * wgrad[:, at : at + 128]
        )
    slots = [
        jnp.concatenate(
            [spread[pl.ds(j * ROWS + slot, 12, stride=4), :] for j in range(WIDE // 128)], axis=1
        )
        for slot in range(4)
    ]
    pgrad = [slots[i] + slots[j] for i, j in PAIRS]
    share = [probs[p] for p in range(6)]
    mean = share[0] * pgrad[0]
    for p in range(1, 6):
        mean = mean + share[p] * pgrad[p]
    for p in range(6):
        lgrad = share[p] * (pgrad[p] - mean)
        first = beta_one * one[p] + (1.0 - beta_one) * lgrad
        second = beta_two * two[p] + (1.0 - beta_two) * lgrad * lgrad
        new_one[p] = first
        new_two[p] = second
        first_hat = first / (1.0 - beta_one**adam_step)
        second_hat = second / (1.0 - beta_two**adam_step)
        old = logits[p]
        new_logits[p] = old - rate * (first_hat / (jnp.sqrt(second_hat) + adam_eps) + decay * old)


def adam(wgrad, weight, probs, logits, one, two):
    cols = weight.shape[1]
    wide = WIDE
    three = pl.BlockSpec((6, 12, wide), lambda i: (0, 0, i))
    flat = pl.BlockSpec((ROWS, wide), lambda i: (0, i))
    out = jax.ShapeDtypeStruct((6, 12, cols), F32)
    return pl.pallas_call(
        adam_kernel,
        grid=(cols // wide,),
        in_specs=[flat, flat, three, three, three, three],
        out_specs=[three, three, three],
        out_shape=[out, out, out],
        scratch_shapes=[pltpu.VMEM((wide // 128 * ROWS, 128), F32)],
        compiler_params=pltpu.CompilerParams(vmem_limit_bytes=16 * MIB),
        cost_estimate=LIGHT,
    )(wgrad, weight, probs, logits, one, two)


def meet_kernel(place, mine, other, out):
    for i in range(64):
        at = pl.multiple_of(place[i] * ROWS, ROWS)
        out[pl.ds(at, ROWS), :128] = mine[i * ROWS : (i + 1) * ROWS, :]
        out[pl.ds(at, ROWS), 128:] = other[i * ROWS : (i + 1) * ROWS, :]


def meet(place, mine, other):
    return pl.pallas_call(
        meet_kernel,
        in_specs=[pl.BlockSpec(memory_space=pltpu.SMEM)] + [IN_VMEM] * 2,
        out_specs=IN_VMEM,
        out_shape=jax.ShapeDtypeStruct((3072, 256), BF16),
        compiler_params=pltpu.CompilerParams(vmem_limit_bytes=16 * MIB),
        cost_estimate=LIGHT,
    )(place, mine, other)


BLOCKS = (
    (*range(0, 16), *range(24, 32), *range(16, 24)),
    (*range(32, 48), *range(56, 64), *range(48, 56)),
)


def fold_kernel(place, *refs):
    keep, give, total = refs[-3:]
    for group, blocks in enumerate(BLOCKS):
        for i, block in enumerate(blocks):
            at = pl.multiple_of(place[block] * ROWS, ROWS)
            total[pl.ds(at, ROWS), :] = refs[group][i * ROWS : (i + 1) * ROWS, :]
    for group, blocks in enumerate(BLOCKS):
        for i, block in enumerate(blocks):
            at = pl.multiple_of(place[64 + block] * ROWS, ROWS)
            rows = pl.ds(at, ROWS)
            total[rows, :] = total[rows, :] + refs[2 + group][i * ROWS : (i + 1) * ROWS, :]
    keep[...] = total[:1536, :]
    give[...] = total[1536:, :]


def half_kernel(place, mine, other, keep, give):
    at = pl.multiple_of(place[0] * 768, 768)
    keep[...] = mine[pl.ds(at, 768), :] + other[pl.ds(at, 768), :]
    at = pl.multiple_of((1 - place[0]) * 768, 768)
    give[...] = mine[pl.ds(at, 768), :] + other[pl.ds(at, 768), :]


def fold(kernel, place, rows, *parts, scratch=()):
    out = jax.ShapeDtypeStruct((rows, 128), F32)
    return pl.pallas_call(
        kernel,
        in_specs=[pl.BlockSpec(memory_space=pltpu.SMEM)] + [IN_VMEM] * len(parts),
        out_specs=[IN_VMEM] * 2,
        out_shape=[out, out],
        scratch_shapes=scratch,
        compiler_params=pltpu.CompilerParams(vmem_limit_bytes=16 * MIB),
        cost_estimate=LIGHT,
    )(place.astype(jnp.int32), *parts)


def share(acts, cot, start, count, at):
    return dot(acts[start : start + count, :], cot[:, at : at + TILE], ((1,), (0,)))


def stack_kernel(*refs):
    out, at = refs[-1], 0
    for ref in refs[:-1]:
        out[at : at + ref.shape[0], :] = ref[...]
        at += ref.shape[0]


def lead(acts, cot, start, base, up, down):
    for at in range(0, HALF, TILE):
        cols = slice(at, at + TILE)
        up[base : base + 192, cols] = share(acts, cot, start, 192, at).astype(BF16)
        down[base : base + 192, cols] = share(acts, cot, start + 192, 192, at).astype(BF16)


def follow(acts, cot, start_up, start_down, low, high, base, up, down):
    for at in range(0, HALF, TILE):
        cols = slice(at, at + TILE)
        got = share(acts, cot, start_up, 192, at) + low[base : base + 192, cols].astype(F32)
        up[:192, cols] = got.astype(BF16)
        up[192:384, cols] = share(acts, cot, start_up + 192, 192, at).astype(BF16)
        down[:192, cols] = share(acts, cot, start_down, 192, at).astype(BF16)
        got = share(acts, cot, start_down + 192, 192, at) + high[base : base + 192, cols].astype(F32)
        down[192:384, cols] = got.astype(BF16)


def second_kernel(start, acts, cot, near, far, up, down):
    up[:192, :] = far[192:384, :]
    down[:192, :] = near[:192, :]
    lead(acts, cot, start, 192, up, down)


def third_kernel(start_up, start_down, acts, cot, low, high, up, down):
    follow(acts, cot, start_up, start_down, low, high, 192, up, down)


def sum_kernel(own, one, two, three, out):
    total = own[...] + one[...].astype(F32) + two[...].astype(F32) + three[...].astype(F32)
    out[...] = total.astype(out.dtype)


def keep_kernel(start, acts, cot, up, down, own, *others):
    for at in range(0, HALF, TILE):
        cols = slice(at, at + TILE)
        for i in range(4):
            rows = slice(i * 96, i * 96 + 96)
            got = share(acts, cot, start + i * 96, 96, at)
            got = got + up[rows, cols].astype(F32) + down[rows, cols].astype(F32)
            if i == 0:
                own[:, cols] = got
            else:
                others[i - 1][:, cols] = got.astype(BF16)


def in_vmem(kernel, out_shape, *args, after=(), cost=LIGHT):
    if after:
        inner, count, kept = kernel, len(args), len(args) + len(after)

        def kernel(*refs):
            inner(*refs[:count], *refs[kept:])

        args = args + tuple(after)
    return pl.pallas_call(
        kernel,
        in_specs=[IN_VMEM] * len(args),
        out_specs=[IN_VMEM] * len(out_shape),
        out_shape=out_shape,
        compiler_params=pltpu.CompilerParams(vmem_limit_bytes=24 * MIB),
        cost_estimate=cost,
    )(*args)


def shape16(rows):
    return jax.ShapeDtypeStruct((rows, HALF), BF16)


def product_kernel(spans, first, joined, acts, cot, *refs):
    size = len(spans)
    before = None if first else refs[0]
    refs = refs if first else refs[1:]
    pieces, (result, mine, theirs) = refs[:size], refs[-3:]
    for at in range(0, HALF, TILE):
        cols = slice(at, at + TILE)
        total = None if first else before[:, cols]
        for (start, skip, count), piece in zip(spans, pieces):
            rows = piece[skip : skip + count, cols]
            term = dot(acts[start : start + count, :], rows, ((0,), (0,)))
            total = term if total is None else total + term
        result[:, cols] = total.astype(result.dtype)
    at = 0
    if joined:
        at = refs[size].shape[0]
        mine[:at, :] = refs[size][...]
        theirs[:at, :] = refs[size + 1][...]
    for (start, skip, count), piece in zip(spans, pieces):
        grad = dot(piece[skip : skip + count, :], cot[...], ((1,), (1,)))
        mine[at : at + count, :] = grad[:, :128]
        theirs[at : at + count, :] = grad[:, 128:]
        at += count


def products(acts, cot, before, parts, after, cost=HEAVY, kind=F32, joined=()):
    first = before is None
    spans = [p[:3] for p in parts]
    rows = sum(p[2] for p in parts) + (joined[0].shape[0] if joined else 0)
    columns = jax.ShapeDtypeStruct((rows, 128), F32)
    shapes = [jax.ShapeDtypeStruct((256, HALF), kind), columns, columns]
    args = [acts, cot] + ([] if first else [before]) + [p[3] for p in parts] + list(joined)
    kernel = functools.partial(product_kernel, spans, first, bool(joined))
    return in_vmem(kernel, shapes, *args, after=after, cost=cost)


def local(tokens, weight, logits, gumbel, cotangent, moment_one, moment_two):
    dp = lax.axis_index("dp")
    mp = lax.axis_index("mp")
    core, y, x, zh = dp % 2, (dp // 2) % 4, (dp // 8) % 4, dp // 32

    def half(value, which):
        return lax.dynamic_slice_in_dim(value, which * HALF, HALF, axis=1)

    whole = np.arange(64)
    dx, dy = (whole // 8 - x) % 4, (whole // 2 - y) % 4
    da, db = jnp.where(core == 0, dx, dy), jnp.where(core == 0, dy, dx)
    met_at = ((((whole // 32) ^ zh) * 4 + db) * 4 + da) * 2 + ((whole % 2) ^ core)
    met_at = met_at.astype(jnp.int32)
    order = np.arange(64)
    oz, ob, oa, oc = order // 32, (order // 8) % 4, (order // 2) % 4, order % 2

    def folded_at(side):
        ox, oy = jnp.where(side == 0, oa, ob), jnp.where(side == 0, ob, oa)
        block = (((oz ^ zh) * 4 + (ox + x) % 4) * 4 + (oy + y) % 4) * 2 + (oc ^ side)
        quarter = block // 16
        return ((((quarter % 2) ^ (mp % 2)) * 2 + quarter // 2) * 16) + block % 16


    flipped = tokens.T
    crossed_x = send(flipped, crossed(1))
    probs, masked = make_masked(logits, gumbel, weight)
    block = in_vmem(
        stack_kernel, [shape16(96)],
        half(masked, core), send(half(masked, 1 - core), SIBLING), after=(crossed_x,),
    )[0]
    blocks = [block, send(block, PARTNER)]

    def start_of(dz, db):
        return (dz * 4 + db) * 384

    def spread_a(mine):
        return [mine, send(mine, A_DOWN), send(mine, A_TWO), send(mine, A_UP)]

    def kept(dz, up, down, after):
        own, one, two, three = in_vmem(
            functools.partial(keep_kernel, start_of(dz, 0)),
            [jax.ShapeDtypeStruct((96, HALF), F32)] + [shape16(96)] * 3, acts, cot, up, down,
            after=after,
        )
        return own, send(one, A_UP), send(two, A_TWO), send(three, A_DOWN)

    cot = jnp.concatenate(
        [half(cotangent, core), send(half(cotangent, 1 - core), SIBLING)], axis=0
    )
    line0 = in_vmem(
        stack_kernel, [shape16(384)], *spread_a(blocks[0]), after=(blocks[1], cot)
    )[0]
    near0, far0 = send(line0, B_DOWN), send(line0, B_UP)
    own = in_vmem(
        stack_kernel, [jax.ShapeDtypeStruct((1536, 128), BF16)], flipped, crossed_x, after=(line0,)
    )[0]
    line1 = in_vmem(stack_kernel, [shape16(384)], *spread_a(blocks[1]))[0]
    near1, far1 = send(line1, B_DOWN), send(line1, B_UP)
    whole_x = in_vmem(
        stack_kernel, [jax.ShapeDtypeStruct((3072, 128), BF16)],
        own, send(own, crossed(2)), after=(line1,),
    )[0]

    came = jnp.concatenate([(mp ^ r) * 16 + np.arange(16) for r in range(4)])
    acts = meet(met_at[came], whole_x, send(whole_x, SIBLING))
    up2, down2 = in_vmem(
        functools.partial(second_kernel, start_of(1, 2)),
        [shape16(384)] * 2, acts, cot, near0, far0, after=(line1,),
    )
    high0, low0 = send(up2, B_UP), send(down2, B_DOWN)
    result, *grad_a = products(
        acts, cot, None,
        [
            (start_of(0, 0), 0, 384, line0),
            (start_of(0, 1), 0, 384, near0),
            (start_of(0, 3), 0, 384, far0),
        ],
        (up2,),
    )
    up3, down3 = in_vmem(
        functools.partial(second_kernel, start_of(0, 2)),
        [shape16(384)] * 2, acts, cot, near1, far1, after=(result,),
    )
    result, *grad_c = products(
        acts, cot, result,
        [
            (start_of(1, 0), 0, 384, line1),
            (start_of(1, 1), 0, 384, near1),
            (start_of(1, 3), 0, 384, far1),
        ],
        (up3,),
    )
    high1, low1 = send(up3, B_UP), send(down3, B_DOWN)
    up4, down4 = in_vmem(
        functools.partial(third_kernel, start_of(1, 1), start_of(1, 3)),
        [shape16(384)] * 2, acts, cot, high0, low0, after=(result,),
    )
    result, *grad_b = products(
        acts, cot, result,
        [(start_of(0, 2), 0, 192, low0), (start_of(0, 2) + 192, 0, 192, high0)],
        (up4,), LIGHT, joined=grad_a,
    )
    up4, down4 = send(up4, B_UP), send(down4, B_DOWN)
    up5, down5 = in_vmem(
        functools.partial(third_kernel, start_of(0, 1), start_of(0, 3)),
        [shape16(384)] * 2, acts, cot, high1, low1,
        after=(grad_b[0],),
    )
    result, *grad_d = products(
        acts, cot, result,
        [(start_of(1, 2), 0, 192, low1), (start_of(1, 2) + 192, 0, 192, high1)],
        (up4,), LIGHT, BF16, grad_c,
    )
    up5, down5 = send(up5, B_UP), send(down5, B_DOWN)
    keep, give = fold(
        fold_kernel, jnp.concatenate([folded_at(core), folded_at(1 - core)]), 1536,
        grad_b[0], grad_d[0], send(grad_b[1], SIBLING), send(grad_d[1], SIBLING),
        scratch=[pltpu.VMEM((3072, 128), F32)],
    )
    own_part, give = fold(
        half_kernel, jnp.reshape(mp // 2, (1,)), 768, keep, send(give, crossed(1))
    )
    total = own_part + send(give, crossed(2))

    sums = in_vmem(sum_kernel, [shape16(96)], *kept(1, up4, down4, ()))
    sums += in_vmem(
        sum_kernel,
        [jax.ShapeDtypeStruct((96, HALF), F32)], *kept(0, up5, down5, (sums[0],)),
        after=(own_part,),
    )
    wsum = sums[1] + send(sums[0], PARTNER).astype(F32)
    other = send(wsum[ROWS:], SIBLING)
    wgrad = jnp.where(
        core == 0,
        jnp.concatenate([wsum[:ROWS], other], axis=1),
        jnp.concatenate([other, wsum[:ROWS]], axis=1),
    )
    new_logits, new_one, new_two = adam(wgrad, weight, probs, logits, moment_one, moment_two)

    other = send(result[128:], SIBLING)
    output = jnp.where(
        core == 0,
        jnp.concatenate([result[:128], other], axis=1),
        jnp.concatenate([other, result[:128]], axis=1),
    )

    input_grad = total.astype(BF16).T
    return (output, input_grad, new_logits, new_one, new_two)


def solution(mesh):
    placed = (
        P("dp", "mp"),
        P("dp", "mp"),
        P(None, "dp", "mp"),
        P(None, "dp", "mp"),
        P("dp", "mp"),
        P(None, "dp", "mp"),
        P(None, "dp", "mp"),
    )
    return jax.shard_map(
        local,
        mesh=mesh,
        in_specs=placed,
        out_specs=(
            P("dp", "mp"),
            P("dp", "mp"),
            P(None, "dp", "mp"),
            P(None, "dp", "mp"),
            P(None, "dp", "mp"),
        ),
        check_vma=False,
    )
```

profile of v0, /device:TPU:1, one launch (start us, length us, event | category | flops | bytes accessed | tf_op | source)
XLA Modules:
  0.0 177.6 jit_solution(4575750827255060029)
XLA Ops:
  1.7 2.6 %collective-permute-start = (bf16[768,128]{1,0:T(8,128)(2,1)S(1)}, bf16[768,128]{1,0:T(8,128)(2,1)S(1)}, u32[]{:S(2)}, u32[]{:S(2)}) collective-permute-start(bf16[768,128]{1,0:T(8,128)(2,1)S(1)} %bitcast.14), channel_id=1, source_target_pairs={{0,1},{1,0},{2,3},{3,2},{4,5},{5,4},{6,7},{7,6},{8,9},{9,8},{10,11... | collective-permute-start | bytes 589832 | tf_op jit(solution)/shard_map/ppermute | solution.py:70
  4.3 1.3 copy-done
  10.6 6.1 %collective-permute-start.5 = (bf16[96,1536]{1,0:T(8,128)(2,1)S(1)}, bf16[96,1536]{1,0:T(8,128)(2,1)S(1)}, u32[]{:S(2)}, u32[]{:S(2)}) collective-permute-start(bf16[96,1536]{1,0:T(8,128)(2,1)S(1)} %shard_map.219.refs_0_), channel_id=1, source_target_pairs={{0,128},{1,129},{2,130},{3,131},{4,132},{5,133},{6,134},{7,135},{8... | collective-permute-start | bytes 884744 | tf_op jit(solution)/shard_map/ppermute | solution.py:70
  16.7 1.3 collective-permute-start.4
  18.0 2.6 %collective-permute-start.3 = (bf16[96,1536]{1,0:T(8,128)(2,1)S(1)}, bf16[96,1536]{1,0:T(8,128)(2,1)S(1)}, u32[]{:S(2)}, u32[]{:S(2)}) collective-permute-start(bf16[96,1536]{1,0:T(8,128)(2,1)S(1)} %shard_map.219.refs_0_), channel_id=1, source_target_pairs={{0,64},{1,65},{2,66},{3,67},{4,20},{5,21},{6,22},{7,23},{8,72},{9,... | collective-permute-start | bytes 884744 | tf_op jit(solution)/shard_map/ppermute | solution.py:70
  21.7 3.1 %collective-permute-done.5.refs_4_.refs_0_ = bf16[96,1536]{1,0:T(8,128)(2,1)S(1)} collective-permute-done((bf16[96,1536]{1,0:T(8,128)(2,1)S(1)}, bf16[96,1536]{1,0:T(8,128)(2,1)S(1)}, u32[]{:S(2)}, u32[]{:S(2)}) %collective-permute-start.5) | collective-permute-done | bytes 294944 | tf_op jit(solution)/shard_map/ppermute | solution.py:70
  24.8 1.3 collective-permute-start.10
  26.2 2.0 %collective-permute-done.3.refs_2_ = bf16[96,1536]{1,0:T(8,128)(2,1)S(1)} collective-permute-done((bf16[96,1536]{1,0:T(8,128)(2,1)S(1)}, bf16[96,1536]{1,0:T(8,128)(2,1)S(1)}, u32[]{:S(2)}, u32[]{:S(2)}) %collective-permute-start.3) | collective-permute-done | bytes 294944 | tf_op jit(solution)/shard_map/ppermute | solution.py:70
  29.3 1.3 shard_map.221.refs_0_
  30.6 5.9 %collective-permute-start.7 = (bf16[1536,128]{1,0:T(8,128)(2,1)S(1)}, bf16[1536,128]{1,0:T(8,128)(2,1)S(1)}, u32[]{:S(2)}, u32[]{:S(2)}) collective-permute-start(bf16[1536,128]{1,0:T(8,128)(2,1)S(1)} %shard_map.221.refs_0_), channel_id=1, source_target_pairs={{0,2},{1,3},{2,0},{3,1},{4,6},{5,7},{6,4},{7,5},{8,10},{9,11},{10,... | collective-permute-start | bytes 1179656 | tf_op jit(solution)/shard_map/ppermute | solution.py:70
  36.5 1.2 collective-permute-start.13
  37.7 1.5 collective-permute-start.12
  39.2 2.6 %collective-permute-start.9 = (bf16[96,1536]{1,0:T(8,128)(2,1)S(1)}, bf16[96,1536]{1,0:T(8,128)(2,1)S(1)}, u32[]{:S(2)}, u32[]{:S(2)}) collective-permute-start(bf16[96,1536]{1,0:T(8,128)(2,1)S(1)} %collective-permute-done.5.refs_4_.refs_0_), channel_id=1, source_target_pairs={{0,64},{1,65},{2,66},{3,67},{4,20},{5,21},{6,22},{7,23},{8,72},{9,... | collective-permute-start | bytes 884744 | tf_op jit(solution)/shard_map/ppermute | solution.py:70
  42.9 6.8 %collective-permute-done.9.refs_2_ = bf16[96,1536]{1,0:T(8,128)(2,1)S(1)} collective-permute-done((bf16[96,1536]{1,0:T(8,128)(2,1)S(1)}, bf16[96,1536]{1,0:T(8,128)(2,1)S(1)}, u32[]{:S(2)}, u32[]{:S(2)}) %collective-permute-start.9) | collective-permute-done | bytes 294944 | tf_op jit(solution)/shard_map/ppermute | solution.py:70
  49.7 5.4 %collective-permute-done.8.refs_1_ = bf16[96,1536]{1,0:T(8,128)(2,1)S(1)} collective-permute-done((bf16[96,1536]{1,0:T(8,128)(2,1)S(1)}, bf16[96,1536]{1,0:T(8,128)(2,1)S(1)}, u32[]{:S(2)}, u32[]{:S(2)}) %collective-permute-start.8) | collective-permute-done | bytes 294944 | tf_op jit(solution)/shard_map/ppermute | solution.py:70
  55.2 2.7 %collective-permute-start.11 = (bf16[3072,128]{1,0:T(8,128)(2,1)S(1)}, bf16[3072,128]{1,0:T(8,128)(2,1)S(1)}, u32[]{:S(2)}, u32[]{:S(2)}) collective-permute-start(bf16[3072,128]{1,0:T(8,128)(2,1)S(1)} %shard_map.223.mine), channel_id=1, source_target_pairs={{0,4},{1,5},{2,6},{3,7},{4,0},{5,1},{6,2},{7,3},{8,12},{9,13},{10,... | collective-permute-start | bytes 2359304 | tf_op jit(solution)/shard_map/ppermute | solution.py:70
  58.9 1.3 fusion.3
  61.1 2.7 %collective-permute-start.14 = (bf16[384,1536]{1,0:T(8,128)(2,1)S(1)}, bf16[384,1536]{1,0:T(8,128)(2,1)S(1)}, u32[]{:S(2)}, u32[]{:S(2)}) collective-permute-start(bf16[384,1536]{1,0:T(8,128)(2,1)S(1)} %shard_map.222.refs_2_.refs_4_.refs_3_), channel_id=1, source_target_pairs={{0,24},{1,25},{2,26},{3,27},{4,100},{5,101},{6,102},{7,103},{8,0},... | collective-permute-start | bytes 3538952 | tf_op jit(solution)/shard_map/ppermute | solution.py:70
  67.8 2.2 %shard_map.225 = (bf16[384,1536]{1,0:T(8,128)(2,1)S(1)}, bf16[384,1536]{1,0:T(8,128)(2,1)S(1)}) custom-call(bf16[3072,256]{1,0:T(8,128)(2,1)S(1)} %shard_map.224.refs_0_.acts, bf16[256,1536]{1,0:T(8,128)(2,1)S(1)} %pad_maximum_fusion.refs_5_.refs_1_.cot, bf16[384,1536]{1,0:T(8,128)(2,1)} %collective-permute-done.12.refs_2_.refs_3_, ...), custom_call_target="tpu_custom_call" | custom-call | bytes 1 | tf_op jit(solution)/shard_map/pallas_call | solution.py:292
  71.5 4.3 %shard_map.226 = (f32[256,1536]{1,0:T(8,128)S(1)}, f32[1152,128]{1,0:T(8,128)S(1)}, f32[1152,128]{1,0:T(8,128)S(1)}) custom-call(bf16[3072,256]{1,0:T(8,128)(2,1)S(1)} %shard_map.224.refs_0_.acts, bf16[256,1536]{1,0:T(8,128)(2,1)S(1)} %pad_maximum_fusion.refs_5_.refs_1_.cot, bf16[384,1536]{1,0:T(8,128)(2,1)} %shard_map.220.refs_2_, ...), custom_call_target="tpu_custom_call" | custom-call | flops 20000000000 | bytes 1 | tf_op jit(solution)/shard_map/pallas_call | solution.py:292
  75.8 1.9 %collective-permute-done.15.refs_3_.refs_5_ = bf16[384,1536]{1,0:T(8,128)(2,1)S(1)} collective-permute-done((bf16[384,1536]{1,0:T(8,128)(2,1)S(1)}, bf16[384,1536]{1,0:T(8,128)(2,1)S(1)}, u32[]{:S(2)}, u32[]{:S(2)}) %collective-permute-start.15) | collective-permute-done | bytes 1179680 | tf_op jit(solution)/shard_map/ppermute | solution.py:70
  78.2 2.8 %collective-permute-start.18 = (bf16[384,1536]{1,0:T(8,128)(2,1)S(1)}, bf16[384,1536]{1,0:T(8,128)(2,1)S(1)}, u32[]{:S(2)}, u32[]{:S(2)}) collective-permute-start(bf16[384,1536]{1,0:T(8,128)(2,1)S(1)} %get-tuple-element.52), channel_id=1, source_target_pairs={{0,24},{1,25},{2,26},{3,27},{4,100},{5,101},{6,102},{7,103},{8,0},... | collective-permute-start | bytes 3538952 | tf_op jit(solution)/shard_map/ppermute | solution.py:70
  81.0 2.3 %shard_map.228 = (f32[256,1536]{1,0:T(8,128)S(1)}, f32[1152,128]{1,0:T(8,128)S(1)}, f32[1152,128]{1,0:T(8,128)S(1)}) custom-call(bf16[3072,256]{1,0:T(8,128)(2,1)S(1)} %shard_map.224.refs_0_.acts, bf16[256,1536]{1,0:T(8,128)(2,1)S(1)} %pad_maximum_fusion.refs_5_.refs_1_.cot, f32[256,1536]{1,0:T(8,128)S(1)} %get-tuple-element.44.refs_4_.refs_2_, ...), custom_call_target="tpu_custom_call" | custom-call | flops 20000000000 | bytes 1 | tf_op jit(solution)/shard_map/pallas_call | solution.py:292
  83.3 6.7 %collective-permute-done.16.refs_3_ = bf16[384,1536]{1,0:T(8,128)(2,1)S(1)} collective-permute-done((bf16[384,1536]{1,0:T(8,128)(2,1)S(1)}, bf16[384,1536]{1,0:T(8,128)(2,1)S(1)}, u32[]{:S(2)}, u32[]{:S(2)}) %collective-permute-start.16) | collective-permute-done | bytes 1179680 | tf_op jit(solution)/shard_map/ppermute | solution.py:70
  91.1 1.3 collective-permute-start.20
  92.4 1.5 collective-permute-start.28
  95.1 7.6 %collective-permute-done.18.refs_3_ = bf16[384,1536]{1,0:T(8,128)(2,1)S(1)} collective-permute-done((bf16[384,1536]{1,0:T(8,128)(2,1)S(1)}, bf16[384,1536]{1,0:T(8,128)(2,1)S(1)}, u32[]{:S(2)}, u32[]{:S(2)}) %collective-permute-start.18) | collective-permute-done | bytes 1179680 | tf_op jit(solution)/shard_map/ppermute | solution.py:70
  102.9 2.1 %shard_map.234 = (bf16[384,1536]{1,0:T(8,128)(2,1)}, bf16[384,1536]{1,0:T(8,128)(2,1)}) custom-call(bf16[3072,256]{1,0:T(8,128)(2,1)S(1)} %shard_map.224.refs_0_.acts, bf16[256,1536]{1,0:T(8,128)(2,1)S(1)} %pad_maximum_fusion.refs_5_.refs_1_.cot, bf16[384,1536]{1,0:T(8,128)(2,1)S(1)} %collective-permute-done.19.refs_4_.refs_2_, ...), custom_call_target="tpu_custom_call" | custom-call | bytes 1 | tf_op jit(solution)/shard_map/pallas_call | solution.py:292
  105.0 1.2 collective-permute-start.26
  106.2 1.5 collective-permute-start.27
  107.7 1.4 collective-permute-start.22
  109.1 6.4 %collective-permute-done.20.refs_7_.up = bf16[384,1536]{1,0:T(8,128)(2,1)S(1)} collective-permute-done((bf16[384,1536]{1,0:T(8,128)(2,1)S(1)}, bf16[384,1536]{1,0:T(8,128)(2,1)S(1)}, u32[]{:S(2)}, u32[]{:S(2)}) %collective-permute-start.20) | collective-permute-done | bytes 1179680 | tf_op jit(solution)/shard_map/ppermute | solution.py:70
  117.7 1.5 shard_map.235
  119.6 1.9 %shard_map.232 = (f32[1536,128]{1,0:T(8,128)S(1)}, f32[1536,128]{1,0:T(8,128)}) custom-call(s32[128]{0:T(128)S(1)} %pad_add_fusion.place, f32[1536,128]{1,0:T(8,128)S(1)} %get-tuple-element.56.refs_0_.refs_4_, f32[1536,128]{1,0:T(8,128)S(1)} %get-tuple-element.57.refs_1_, f32[1536,128]{1,0:T(8,128)S(1)} %collective-permute-done.22.refs_2_, ...), custom_call_target="tpu_custom_call" | custom-call | bytes 1 | tf_op jit(solution)/shard_map/pallas_call | solution.py:216
  122.4 1.5 collective-permute-start.30
  123.9 6.5 %collective-permute-done.29.one = bf16[96,1536]{1,0:T(8,128)(2,1)S(1)} collective-permute-done((bf16[96,1536]{1,0:T(8,128)(2,1)S(1)}, bf16[96,1536]{1,0:T(8,128)(2,1)S(1)}, u32[]{:S(2)}, u32[]{:S(2)}) %collective-permute-start.29) | collective-permute-done | bytes 294944 | tf_op jit(solution)/shard_map/ppermute | solution.py:70
  131.1 3.7 %collective-permute-done.30.two = bf16[96,1536]{1,0:T(8,128)(2,1)} collective-permute-done((bf16[96,1536]{1,0:T(8,128)(2,1)}, bf16[96,1536]{1,0:T(8,128)(2,1)}, u32[]{:S(2)}, u32[]{:S(2)}) %collective-permute-start.30) | collective-permute-done | bytes 294944 | tf_op jit(solution)/shard_map/ppermute | solution.py:70
  134.8 2.5 %collective-permute-done.31.three = bf16[96,1536]{1,0:T(8,128)(2,1)} collective-permute-done((bf16[96,1536]{1,0:T(8,128)(2,1)}, bf16[96,1536]{1,0:T(8,128)(2,1)}, u32[]{:S(2)}, u32[]{:S(2)}) %collective-permute-start.31) | collective-permute-done | bytes 294944 | tf_op jit(solution)/shard_map/ppermute | solution.py:70
  140.5 4.2 %collective-permute-start.35 = (bf16[96,1536]{1,0:T(8,128)(2,1)S(1)}, bf16[96,1536]{1,0:T(8,128)(2,1)S(1)}, u32[]{:S(2)}, u32[]{:S(2)}) collective-permute-start(bf16[96,1536]{1,0:T(8,128)(2,1)S(1)} %shard_map.236.refs_4_), channel_id=1, source_target_pairs={{0,128},{1,129},{2,130},{3,131},{4,132},{5,133},{6,134},{7,135},{8... | collective-permute-start | bytes 884744 | tf_op jit(solution)/shard_map/ppermute | solution.py:70
  144.7 1.9 %shard_map.237 = (f32[96,1536]{1,0:T(8,128)S(1)}, bf16[96,1536]{1,0:T(8,128)(2,1)S(1)}, bf16[96,1536]{1,0:T(8,128)(2,1)S(1)}, bf16[96,1536]{1,0:T(8,128)(2,1)S(1)}) custom-call(bf16[3072,256]{1,0:T(8,128)(2,1)S(1)} %shard_map.224.refs_0_.acts, bf16[256,1536]{1,0:T(8,128)(2,1)S(1)} %pad_maximum_fusion.refs_5_.refs_1_.cot, ...), custom_call_target="tpu_custom_call" | custom-call | bytes 1 | tf_op jit(solution)/shard_map/pallas_call | solution.py:292
  146.8 2.1 %collective-permute-start.33 = (bf16[96,1536]{1,0:T(8,128)(2,1)S(1)}, bf16[96,1536]{1,0:T(8,128)(2,1)S(1)}, u32[]{:S(2)}, u32[]{:S(2)}) collective-permute-start(bf16[96,1536]{1,0:T(8,128)(2,1)S(1)} %get-tuple-element.73), channel_id=1, source_target_pairs={{0,64},{1,65},{2,66},{3,67},{4,20},{5,21},{6,22},{7,23},{8,72},{9,... | collective-permute-start | bytes 884744 | tf_op jit(solution)/shard_map/ppermute | solution.py:70
  149.5 4.0 %collective-permute-start.21 = (bf16[128,1536]{1,0:T(8,128)(2,1)S(1)}, bf16[128,1536]{1,0:T(8,128)(2,1)S(1)}, u32[]{:S(2)}, u32[]{:S(2)}) collective-permute-start(bf16[128,1536]{1,0:T(8,128)(2,1)S(1)} %get-tuple-element.90), channel_id=1, source_target_pairs={{0,4},{1,5},{2,6},{3,7},{4,0},{5,1},{6,2},{7,3},{8,12},{9,13},{10,... | collective-permute-start | bytes 1179656 | tf_op jit(solution)/shard_map/ppermute | solution.py:70
  153.5 1.2 shard_map.233
  154.7 2.3 %collective-permute-done.32.refs_1_ = bf16[96,1536]{1,0:T(8,128)(2,1)S(1)} collective-permute-done((bf16[96,1536]{1,0:T(8,128)(2,1)S(1)}, bf16[96,1536]{1,0:T(8,128)(2,1)S(1)}, u32[]{:S(2)}, u32[]{:S(2)}) %collective-permute-start.32) | collective-permute-done | bytes 294944 | tf_op jit(solution)/shard_map/ppermute | solution.py:70
  157.0 1.4 collective-permute-start.25
  158.7 2.5 %collective-permute-start.36 = (f32[48,1536]{1,0:T(8,128)S(1)}, f32[48,1536]{1,0:T(8,128)S(1)}, u32[]{:S(2)}, u32[]{:S(2)}) collective-permute-start(f32[48,1536]{1,0:T(8,128)S(1)} %get-tuple-element.94), channel_id=1, source_target_pairs={{0,4},{1,5},{2,6},{3,7},{4,0},{5,1},{6,2},{7,3},{8,12},{9,13},{10,... | collective-permute-start | bytes 884744 | tf_op jit(solution)/shard_map/ppermute | solution.py:70
  163.2 3.4 %shard_map.239 = (f32[6,12,3072]{2,1,0:T(8,128)}, f32[6,12,3072]{2,1,0:T(8,128)}, f32[6,12,3072]{2,1,0:T(8,128)}) custom-call(f32[48,3072]{1,0:T(8,128)S(1)} %maximum_select_fusion.1.wgrad, bf16[48,3072]{1,0:T(8,128)(2,1)S(1)} %copy-done.5, f32[6,12,3072]{2,1,0:T(8,128)S(1)} %copy-done.9, f32[6,12,3072]{2,1,0:T(8,128)S(1)} %copy-done.1, ...), custom_call_target="tpu_custom_call" | custom-call | bytes 1 | tf_op jit(solution)/shard_map/pallas_call | solution.py:156
  166.6 10.2 %collective-permute-done.25 = f32[768,128]{1,0:T(8,128)S(1)} collective-permute-done((f32[768,128]{1,0:T(8,128)S(1)}, f32[768,128]{1,0:T(8,128)S(1)}, u32[]{:S(2)}, u32[]{:S(2)}) %collective-permute-start.25) | collective-permute-done | bytes 393248 | tf_op jit(solution)/shard_map/ppermute | solution.py:70
  (118 shorter events, 31.1 us)
Async XLA Ops:
  1.7 8.9 %collective-permute-start = (bf16[768,128]{1,0:T(8,128)(2,1)S(1)}, bf16[768,128]{1,0:T(8,128)(2,1)S(1)}, u32[]{:S(2)}, u32[]{:S(2)}) collective-permute-start(bf16[768,128]{1,0:T(8,128)(2,1)S(1)} %bitcast.14), channel_id=1, source_target_pairs={{0,1},{1,0},{2,3},{3,2},{4,5},{5,4},{6,7},{7,6},{8,9},{9,8},{10,11... | collective-permute-start | bytes 589832 | tf_op jit(solution)/shard_map/ppermute | solution.py:70
  8.5 2.1 %copy-start.8 = (f32[6,12,3072]{2,1,0:T(8,128)}, f32[6,12,3072]{2,1,0:T(8,128)S(1)}, u32[]{:S(2)}) copy-start(f32[6,12,3072]{2,1,0:T(8,128)S(1)} %get-tuple-element.75.probs) | copy-start | bytes 2654212
  8.6 2.0 %collective-permute-start.1 = (bf16[48,1536]{1,0:T(8,128)(2,1)S(1)}, bf16[48,1536]{1,0:T(8,128)(2,1)S(1)}, u32[]{:S(2)}, u32[]{:S(2)}) collective-permute-start(bf16[48,1536]{1,0:T(8,128)(2,1)S(1)} %get-tuple-element.95), channel_id=1, source_target_pairs={{0,4},{1,5},{2,6},{3,7},{4,0},{5,1},{6,2},{7,3},{8,12},{9,13},{10,... | collective-permute-start | bytes 442376 | tf_op jit(solution)/shard_map/ppermute | solution.py:70
  9.7 16.5 %collective-permute-start.6 = (bf16[128,1536]{1,0:T(8,128)(2,1)S(1)}, bf16[128,1536]{1,0:T(8,128)(2,1)S(1)}, u32[]{:S(2)}, u32[]{:S(2)}) collective-permute-start(bf16[128,1536]{1,0:T(8,128)(2,1)S(1)} %get-tuple-element.92), channel_id=1, source_target_pairs={{0,4},{1,5},{2,6},{3,7},{4,0},{5,1},{6,2},{7,3},{8,12},{9,13},{10,... | collective-permute-start | bytes 1179656 | tf_op jit(solution)/shard_map/ppermute | solution.py:70
  10.6 14.2 %collective-permute-start.5 = (bf16[96,1536]{1,0:T(8,128)(2,1)S(1)}, bf16[96,1536]{1,0:T(8,128)(2,1)S(1)}, u32[]{:S(2)}, u32[]{:S(2)}) collective-permute-start(bf16[96,1536]{1,0:T(8,128)(2,1)S(1)} %shard_map.219.refs_0_), channel_id=1, source_target_pairs={{0,128},{1,129},{2,130},{3,131},{4,132},{5,133},{6,134},{7,135},{8... | collective-permute-start | bytes 884744 | tf_op jit(solution)/shard_map/ppermute | solution.py:70
  16.7 9.4 %collective-permute-start.4 = (bf16[96,1536]{1,0:T(8,128)(2,1)S(1)}, bf16[96,1536]{1,0:T(8,128)(2,1)S(1)}, u32[]{:S(2)}, u32[]{:S(2)}) collective-permute-start(bf16[96,1536]{1,0:T(8,128)(2,1)S(1)} %shard_map.219.refs_0_), channel_id=1, source_target_pairs={{0,32},{1,33},{2,34},{3,35},{4,12},{5,13},{6,14},{7,15},{8,40},{9,... | collective-permute-start | bytes 884744 | tf_op jit(solution)/shard_map/ppermute | solution.py:70
  18.0 10.2 %collective-permute-start.3 = (bf16[96,1536]{1,0:T(8,128)(2,1)S(1)}, bf16[96,1536]{1,0:T(8,128)(2,1)S(1)}, u32[]{:S(2)}, u32[]{:S(2)}) collective-permute-start(bf16[96,1536]{1,0:T(8,128)(2,1)S(1)} %shard_map.219.refs_0_), channel_id=1, source_target_pairs={{0,64},{1,65},{2,66},{3,67},{4,20},{5,21},{6,22},{7,23},{8,72},{9,... | collective-permute-start | bytes 884744 | tf_op jit(solution)/shard_map/ppermute | solution.py:70
  20.6 7.6 %collective-permute-start.2 = (bf16[96,1536]{1,0:T(8,128)(2,1)S(1)}, bf16[96,1536]{1,0:T(8,128)(2,1)S(1)}, u32[]{:S(2)}, u32[]{:S(2)}) collective-permute-start(bf16[96,1536]{1,0:T(8,128)(2,1)S(1)} %shard_map.219.refs_0_), channel_id=1, source_target_pairs={{0,96},{1,97},{2,98},{3,99},{4,28},{5,29},{6,30},{7,31},{8,104},{9... | collective-permute-start | bytes 884744 | tf_op jit(solution)/shard_map/ppermute | solution.py:70
  24.8 17.0 %collective-permute-start.10 = (bf16[96,1536]{1,0:T(8,128)(2,1)S(1)}, bf16[96,1536]{1,0:T(8,128)(2,1)S(1)}, u32[]{:S(2)}, u32[]{:S(2)}) collective-permute-start(bf16[96,1536]{1,0:T(8,128)(2,1)S(1)} %collective-permute-done.5.refs_4_.refs_0_), channel_id=1, source_target_pairs={{0,32},{1,33},{2,34},{3,35},{4,12},{5,13},{6,14},{7,15},{8,40},{9,... | collective-permute-start | bytes 884744 | tf_op jit(solution)/shard_map/ppermute | solution.py:70
  30.6 24.6 %collective-permute-start.7 = (bf16[1536,128]{1,0:T(8,128)(2,1)S(1)}, bf16[1536,128]{1,0:T(8,128)(2,1)S(1)}, u32[]{:S(2)}, u32[]{:S(2)}) collective-permute-start(bf16[1536,128]{1,0:T(8,128)(2,1)S(1)} %shard_map.221.refs_0_), channel_id=1, source_target_pairs={{0,2},{1,3},{2,0},{3,1},{4,6},{5,7},{6,4},{7,5},{8,10},{9,11},{10,... | collective-permute-start | bytes 1179656 | tf_op jit(solution)/shard_map/ppermute | solution.py:70
  36.5 31.3 %collective-permute-start.13 = (bf16[384,1536]{1,0:T(8,128)(2,1)}, bf16[384,1536]{1,0:T(8,128)(2,1)}, u32[]{:S(2)}, u32[]{:S(2)}) collective-permute-start(bf16[384,1536]{1,0:T(8,128)(2,1)} %shard_map.220.refs_2_), channel_id=1, source_target_pairs={{0,8},{1,9},{2,10},{3,11},{4,36},{5,37},{6,38},{7,39},{8,16},{9,17... | collective-permute-start | bytes 3538952 | tf_op jit(solution)/shard_map/ppermute | solution.py:70
  37.7 30.1 %collective-permute-start.12 = (bf16[384,1536]{1,0:T(8,128)(2,1)}, bf16[384,1536]{1,0:T(8,128)(2,1)}, u32[]{:S(2)}, u32[]{:S(2)}) collective-permute-start(bf16[384,1536]{1,0:T(8,128)(2,1)} %shard_map.220.refs_2_), channel_id=1, source_target_pairs={{0,24},{1,25},{2,26},{3,27},{4,100},{5,101},{6,102},{7,103},{8,0},... | collective-permute-start | bytes 3538952 | tf_op jit(solution)/shard_map/ppermute | solution.py:70
  39.2 10.5 %collective-permute-start.9 = (bf16[96,1536]{1,0:T(8,128)(2,1)S(1)}, bf16[96,1536]{1,0:T(8,128)(2,1)S(1)}, u32[]{:S(2)}, u32[]{:S(2)}) collective-permute-start(bf16[96,1536]{1,0:T(8,128)(2,1)S(1)} %collective-permute-done.5.refs_4_.refs_0_), channel_id=1, source_target_pairs={{0,64},{1,65},{2,66},{3,67},{4,20},{5,21},{6,22},{7,23},{8,72},{9,... | collective-permute-start | bytes 884744 | tf_op jit(solution)/shard_map/ppermute | solution.py:70
  41.8 13.3 %collective-permute-start.8 = (bf16[96,1536]{1,0:T(8,128)(2,1)S(1)}, bf16[96,1536]{1,0:T(8,128)(2,1)S(1)}, u32[]{:S(2)}, u32[]{:S(2)}) collective-permute-start(bf16[96,1536]{1,0:T(8,128)(2,1)S(1)} %collective-permute-done.5.refs_4_.refs_0_), channel_id=1, source_target_pairs={{0,96},{1,97},{2,98},{3,99},{4,28},{5,29},{6,30},{7,31},{8,104},{9... | collective-permute-start | bytes 884744 | tf_op jit(solution)/shard_map/ppermute | solution.py:70
  55.1 3.8 %copy-start.22 = (s32[64]{0:T(128)S(1)}, s32[64]{0:T(128)}, u32[]{:S(2)}) copy-start(s32[64]{0:T(128)} %constant.203.clone) | copy-start | bytes 772
  55.2 3.8 %copy-start.23 = (s32[64]{0:T(128)S(1)}, s32[64]{0:T(128)}, u32[]{:S(2)}) copy-start(s32[64]{0:T(128)} %constant.202.clone) | copy-start | bytes 772
  55.2 8.5 %collective-permute-start.11 = (bf16[3072,128]{1,0:T(8,128)(2,1)S(1)}, bf16[3072,128]{1,0:T(8,128)(2,1)S(1)}, u32[]{:S(2)}, u32[]{:S(2)}) collective-permute-start(bf16[3072,128]{1,0:T(8,128)(2,1)S(1)} %shard_map.223.mine), channel_id=1, source_target_pairs={{0,4},{1,5},{2,6},{3,7},{4,0},{5,1},{6,2},{7,3},{8,12},{9,13},{10,... | collective-permute-start | bytes 2359304 | tf_op jit(solution)/shard_map/ppermute | solution.py:70
  61.0 16.6 %collective-permute-start.15 = (bf16[384,1536]{1,0:T(8,128)(2,1)S(1)}, bf16[384,1536]{1,0:T(8,128)(2,1)S(1)}, u32[]{:S(2)}, u32[]{:S(2)}) collective-permute-start(bf16[384,1536]{1,0:T(8,128)(2,1)S(1)} %shard_map.222.refs_2_.refs_4_.refs_3_), channel_id=1, source_target_pairs={{0,8},{1,9},{2,10},{3,11},{4,36},{5,37},{6,38},{7,39},{8,16},{9,17... | collective-permute-start | bytes 3538952 | tf_op jit(solution)/shard_map/ppermute | solution.py:70
  61.1 16.5 %collective-permute-start.14 = (bf16[384,1536]{1,0:T(8,128)(2,1)S(1)}, bf16[384,1536]{1,0:T(8,128)(2,1)S(1)}, u32[]{:S(2)}, u32[]{:S(2)}) collective-permute-start(bf16[384,1536]{1,0:T(8,128)(2,1)S(1)} %shard_map.222.refs_2_.refs_4_.refs_3_), channel_id=1, source_target_pairs={{0,24},{1,25},{2,26},{3,27},{4,100},{5,101},{6,102},{7,103},{8,0},... | collective-permute-start | bytes 3538952 | tf_op jit(solution)/shard_map/ppermute | solution.py:70
  70.0 20.1 %collective-permute-start.16 = (bf16[384,1536]{1,0:T(8,128)(2,1)S(1)}, bf16[384,1536]{1,0:T(8,128)(2,1)S(1)}, u32[]{:S(2)}, u32[]{:S(2)}) collective-permute-start(bf16[384,1536]{1,0:T(8,128)(2,1)S(1)} %get-tuple-element.47), channel_id=1, source_target_pairs={{0,24},{1,25},{2,26},{3,27},{4,100},{5,101},{6,102},{7,103},{8,0},... | collective-permute-start | bytes 3538952 | tf_op jit(solution)/shard_map/ppermute | solution.py:70
  70.7 19.6 %collective-permute-start.17 = (bf16[384,1536]{1,0:T(8,128)(2,1)S(1)}, bf16[384,1536]{1,0:T(8,128)(2,1)S(1)}, u32[]{:S(2)}, u32[]{:S(2)}) collective-permute-start(bf16[384,1536]{1,0:T(8,128)(2,1)S(1)} %get-tuple-element.43.refs_5_), channel_id=1, source_target_pairs={{0,8},{1,9},{2,10},{3,11},{4,36},{5,37},{6,38},{7,39},{8,16},{9,17... | collective-permute-start | bytes 3538952 | tf_op jit(solution)/shard_map/ppermute | solution.py:70
  78.2 24.4 %collective-permute-start.18 = (bf16[384,1536]{1,0:T(8,128)(2,1)S(1)}, bf16[384,1536]{1,0:T(8,128)(2,1)S(1)}, u32[]{:S(2)}, u32[]{:S(2)}) collective-permute-start(bf16[384,1536]{1,0:T(8,128)(2,1)S(1)} %get-tuple-element.52), channel_id=1, source_target_pairs={{0,24},{1,25},{2,26},{3,27},{4,100},{5,101},{6,102},{7,103},{8,0},... | collective-permute-start | bytes 3538952 | tf_op jit(solution)/shard_map/ppermute | solution.py:70
  81.0 21.9 %collective-permute-start.19 = (bf16[384,1536]{1,0:T(8,128)(2,1)S(1)}, bf16[384,1536]{1,0:T(8,128)(2,1)S(1)}, u32[]{:S(2)}, u32[]{:S(2)}) collective-permute-start(bf16[384,1536]{1,0:T(8,128)(2,1)S(1)} %get-tuple-element.45.refs_6_), channel_id=1, source_target_pairs={{0,8},{1,9},{2,10},{3,11},{4,36},{5,37},{6,38},{7,39},{8,16},{9,17... | collective-permute-start | bytes 3538952 | tf_op jit(solution)/shard_map/ppermute | solution.py:70
  91.1 24.5 %collective-permute-start.20 = (bf16[384,1536]{1,0:T(8,128)(2,1)S(1)}, bf16[384,1536]{1,0:T(8,128)(2,1)S(1)}, u32[]{:S(2)}, u32[]{:S(2)}) collective-permute-start(bf16[384,1536]{1,0:T(8,128)(2,1)S(1)} %get-tuple-element.50.refs_7_), channel_id=1, source_target_pairs={{0,8},{1,9},{2,10},{3,11},{4,36},{5,37},{6,38},{7,39},{8,16},{9,17... | collective-permute-start | bytes 3538952 | tf_op jit(solution)/shard_map/ppermute | solution.py:70
  92.4 25.3 %collective-permute-start.28 = (bf16[384,1536]{1,0:T(8,128)(2,1)S(1)}, bf16[384,1536]{1,0:T(8,128)(2,1)S(1)}, u32[]{:S(2)}, u32[]{:S(2)}) collective-permute-start(bf16[384,1536]{1,0:T(8,128)(2,1)S(1)} %get-tuple-element.66), channel_id=1, source_target_pairs={{0,24},{1,25},{2,26},{3,27},{4,100},{5,101},{6,102},{7,103},{8,0},... | collective-permute-start | bytes 3538952 | tf_op jit(solution)/shard_map/ppermute | solution.py:70
  105.0 39.7 %collective-permute-start.26 = (bf16[384,1536]{1,0:T(8,128)(2,1)}, bf16[384,1536]{1,0:T(8,128)(2,1)S(1)}, u32[]{:S(2)}, u32[]{:S(2)}) collective-permute-start(bf16[384,1536]{1,0:T(8,128)(2,1)} %get-tuple-element.64), channel_id=1, source_target_pairs={{0,8},{1,9},{2,10},{3,11},{4,36},{5,37},{6,38},{7,39},{8,16},{9,17... | collective-permute-start | bytes 3538952 | tf_op jit(solution)/shard_map/ppermute | solution.py:70
  106.2 38.5 %collective-permute-start.27 = (bf16[384,1536]{1,0:T(8,128)(2,1)}, bf16[384,1536]{1,0:T(8,128)(2,1)}, u32[]{:S(2)}, u32[]{:S(2)}) collective-permute-start(bf16[384,1536]{1,0:T(8,128)(2,1)} %get-tuple-element.65), channel_id=1, source_target_pairs={{0,24},{1,25},{2,26},{3,27},{4,100},{5,101},{6,102},{7,103},{8,0},... | collective-permute-start | bytes 3538952 | tf_op jit(solution)/shard_map/ppermute | solution.py:70
  107.7 11.5 %collective-permute-start.22 = (f32[1536,128]{1,0:T(8,128)S(1)}, f32[1536,128]{1,0:T(8,128)S(1)}, u32[]{:S(2)}, u32[]{:S(2)}) collective-permute-start(f32[1536,128]{1,0:T(8,128)S(1)} %get-tuple-element.58), channel_id=1, source_target_pairs={{0,4},{1,5},{2,6},{3,7},{4,0},{5,1},{6,2},{7,3},{8,12},{9,13},{10,... | collective-permute-start | bytes 2359304 | tf_op jit(solution)/shard_map/ppermute | solution.py:70
  116.7 2.4 %copy-start.10 = (bf16[256,1536]{1,0:T(8,128)(2,1)}, bf16[256,1536]{1,0:T(8,128)(2,1)S(1)}, u32[]{:S(2)}) copy-start(bf16[256,1536]{1,0:T(8,128)(2,1)S(1)} %get-tuple-element.55) | copy-start | bytes 2359300
  116.7 2.5 %copy-start.24 = (s32[64]{0:T(128)S(1)}, s32[64]{0:T(128)}, u32[]{:S(2)}) copy-start(s32[64]{0:T(128)} %get-tuple-element.97) | copy-start | bytes 772
  116.7 2.5 %copy-start.25 = (s32[64]{0:T(128)S(1)}, s32[64]{0:T(128)}, u32[]{:S(2)}) copy-start(s32[64]{0:T(128)} %get-tuple-element.98) | copy-start | bytes 772
  116.7 2.9 %collective-permute-start.23 = (f32[1536,128]{1,0:T(8,128)S(1)}, f32[1536,128]{1,0:T(8,128)S(1)}, u32[]{:S(2)}, u32[]{:S(2)}) collective-permute-start(f32[1536,128]{1,0:T(8,128)S(1)} %get-tuple-element.59), channel_id=1, source_target_pairs={{0,4},{1,5},{2,6},{3,7},{4,0},{5,1},{6,2},{7,3},{8,12},{9,13},{10,... | collective-permute-start | bytes 2359304 | tf_op jit(solution)/shard_map/ppermute | solution.py:70
  119.1 2.3 %copy-start.16 = (f32[96,1536]{1,0:T(8,128)}, f32[96,1536]{1,0:T(8,128)S(1)}, u32[]{:S(2)}) copy-start(f32[96,1536]{1,0:T(8,128)S(1)} %get-tuple-element.67.own) | copy-start | bytes 1769476
  119.1 11.2 %collective-permute-start.29 = (bf16[96,1536]{1,0:T(8,128)(2,1)S(1)}, bf16[96,1536]{1,0:T(8,128)(2,1)S(1)}, u32[]{:S(2)}, u32[]{:S(2)}) collective-permute-start(bf16[96,1536]{1,0:T(8,128)(2,1)S(1)} %get-tuple-element.68), channel_id=1, source_target_pairs={{0,32},{1,33},{2,34},{3,35},{4,12},{5,13},{6,14},{7,15},{8,40},{9,... | collective-permute-start | bytes 884744 | tf_op jit(solution)/shard_map/ppermute | solution.py:70
  122.4 27.1 %collective-permute-start.24 = (f32[1536,128]{1,0:T(8,128)}, f32[1536,128]{1,0:T(8,128)}, u32[]{:S(2)}, u32[]{:S(2)}) collective-permute-start(f32[1536,128]{1,0:T(8,128)} %get-tuple-element.61), channel_id=1, source_target_pairs={{0,1},{1,0},{2,3},{3,2},{4,5},{5,4},{6,7},{7,6},{8,9},{9,8},{10,11... | collective-permute-start | bytes 2359304 | tf_op jit(solution)/shard_map/ppermute | solution.py:70
  122.4 12.4 %collective-permute-start.30 = (bf16[96,1536]{1,0:T(8,128)(2,1)}, bf16[96,1536]{1,0:T(8,128)(2,1)}, u32[]{:S(2)}, u32[]{:S(2)}) collective-permute-start(bf16[96,1536]{1,0:T(8,128)(2,1)} %get-tuple-element.69), channel_id=1, source_target_pairs={{0,64},{1,65},{2,66},{3,67},{4,20},{5,21},{6,22},{7,23},{8,72},{9,... | collective-permute-start | bytes 884744 | tf_op jit(solution)/shard_map/ppermute | solution.py:70
  131.1 6.2 %collective-permute-start.31 = (bf16[96,1536]{1,0:T(8,128)(2,1)}, bf16[96,1536]{1,0:T(8,128)(2,1)}, u32[]{:S(2)}, u32[]{:S(2)}) collective-permute-start(bf16[96,1536]{1,0:T(8,128)(2,1)} %get-tuple-element.70), channel_id=1, source_target_pairs={{0,96},{1,97},{2,98},{3,99},{4,28},{5,29},{6,30},{7,31},{8,104},{9... | collective-permute-start | bytes 884744 | tf_op jit(solution)/shard_map/ppermute | solution.py:70
  140.5 8.9 %copy-start.11 = (bf16[256,1536]{1,0:T(8,128)(2,1)S(1)}, bf16[256,1536]{1,0:T(8,128)(2,1)}, u32[]{:S(2)}) copy-start(bf16[256,1536]{1,0:T(8,128)(2,1)} %copy-done.10) | copy-start | bytes 2359300
  140.5 18.0 %collective-permute-start.35 = (bf16[96,1536]{1,0:T(8,128)(2,1)S(1)}, bf16[96,1536]{1,0:T(8,128)(2,1)S(1)}, u32[]{:S(2)}, u32[]{:S(2)}) collective-permute-start(bf16[96,1536]{1,0:T(8,128)(2,1)S(1)} %shard_map.236.refs_4_), channel_id=1, source_target_pairs={{0,128},{1,129},{2,130},{3,131},{4,132},{5,133},{6,134},{7,135},{8... | collective-permute-start | bytes 884744 | tf_op jit(solution)/shard_map/ppermute | solution.py:70
  146.7 6.8 %copy-start.13 = (f32[1536,128]{1,0:T(8,128)S(1)}, f32[1536,128]{1,0:T(8,128)}, u32[]{:S(2)}) copy-start(f32[1536,128]{1,0:T(8,128)} %copy-done.12) | copy-start | bytes 2359300
  146.7 10.3 %collective-permute-start.32 = (bf16[96,1536]{1,0:T(8,128)(2,1)S(1)}, bf16[96,1536]{1,0:T(8,128)(2,1)S(1)}, u32[]{:S(2)}, u32[]{:S(2)}) collective-permute-start(bf16[96,1536]{1,0:T(8,128)(2,1)S(1)} %get-tuple-element.72), channel_id=1, source_target_pairs={{0,32},{1,33},{2,34},{3,35},{4,12},{5,13},{6,14},{7,15},{8,40},{9,... | collective-permute-start | bytes 884744 | tf_op jit(solution)/shard_map/ppermute | solution.py:70
  146.8 11.6 %collective-permute-start.33 = (bf16[96,1536]{1,0:T(8,128)(2,1)S(1)}, bf16[96,1536]{1,0:T(8,128)(2,1)S(1)}, u32[]{:S(2)}, u32[]{:S(2)}) collective-permute-start(bf16[96,1536]{1,0:T(8,128)(2,1)S(1)} %get-tuple-element.73), channel_id=1, source_target_pairs={{0,64},{1,65},{2,66},{3,67},{4,20},{5,21},{6,22},{7,23},{8,72},{9,... | collective-permute-start | bytes 884744 | tf_op jit(solution)/shard_map/ppermute | solution.py:70
  148.8 9.6 %collective-permute-start.34 = (bf16[96,1536]{1,0:T(8,128)(2,1)S(1)}, bf16[96,1536]{1,0:T(8,128)(2,1)S(1)}, u32[]{:S(2)}, u32[]{:S(2)}) collective-permute-start(bf16[96,1536]{1,0:T(8,128)(2,1)S(1)} %get-tuple-element.74), channel_id=1, source_target_pairs={{0,96},{1,97},{2,98},{3,99},{4,28},{5,29},{6,30},{7,31},{8,104},{9... | collective-permute-start | bytes 884744 | tf_op jit(solution)/shard_map/ppermute | solution.py:70
  149.5 11.7 %collective-permute-start.21 = (bf16[128,1536]{1,0:T(8,128)(2,1)S(1)}, bf16[128,1536]{1,0:T(8,128)(2,1)S(1)}, u32[]{:S(2)}, u32[]{:S(2)}) collective-permute-start(bf16[128,1536]{1,0:T(8,128)(2,1)S(1)} %get-tuple-element.90), channel_id=1, source_target_pairs={{0,4},{1,5},{2,6},{3,7},{4,0},{5,1},{6,2},{7,3},{8,12},{9,13},{10,... | collective-permute-start | bytes 1179656 | tf_op jit(solution)/shard_map/ppermute | solution.py:70
  157.0 19.8 %collective-permute-start.25 = (f32[768,128]{1,0:T(8,128)S(1)}, f32[768,128]{1,0:T(8,128)S(1)}, u32[]{:S(2)}, u32[]{:S(2)}) collective-permute-start(f32[768,128]{1,0:T(8,128)S(1)} %get-tuple-element.63), channel_id=1, source_target_pairs={{0,2},{1,3},{2,0},{3,1},{4,6},{5,7},{6,4},{7,5},{8,10},{9,11},{10,... | collective-permute-start | bytes 1179656 | tf_op jit(solution)/shard_map/ppermute | solution.py:70
  158.5 3.9 %copy-start.9 = (f32[6,12,3072]{2,1,0:T(8,128)S(1)}, f32[6,12,3072]{2,1,0:T(8,128)}, u32[]{:S(2)}) copy-start(f32[6,12,3072]{2,1,0:T(8,128)} %copy-done.8) | copy-start | bytes 2654212
  158.6 3.9 %copy-start.7 = (f32[6,12,3072]{2,1,0:T(8,128)S(1)}, f32[6,12,3072]{2,1,0:T(8,128)}, u32[]{:S(2)}) copy-start(f32[6,12,3072]{2,1,0:T(8,128)} %two.1) | copy-start | bytes 2654212
  158.7 3.7 %collective-permute-start.36 = (f32[48,1536]{1,0:T(8,128)S(1)}, f32[48,1536]{1,0:T(8,128)S(1)}, u32[]{:S(2)}, u32[]{:S(2)}) collective-permute-start(f32[48,1536]{1,0:T(8,128)S(1)} %get-tuple-element.94), channel_id=1, source_target_pairs={{0,4},{1,5},{2,6},{3,7},{4,0},{5,1},{6,2},{7,3},{8,12},{9,13},{10,... | collective-permute-start | bytes 884744 | tf_op jit(solution)/shard_map/ppermute | solution.py:70
  (15 other events, 18.1 us)
where the time goes:
time: 178 us
  waiting for transfers between devices  66.9 us (38%)
  starting transfers between devices  62.4 us (35%)
  Pallas kernels  29.9 us (17%)
  local copies, waits for them, and re-layouts  14.6 us (8%)
  other arithmetic  2.76 us (2%)
    ppermute x37, waiting for transfers between devices, send(): return lax.ppermute(value, AXES, pairs)  66.9 us
    ppermute x37, starting transfers between devices, send(): return lax.ppermute(value, AXES, pairs)  62.4 us
    pallas_call x17, Pallas kernels, in_vmem(): pl.pallas_call(kernel, in_specs=[IN_VMEM] * len(args), out_specs=[IN_VMEM...  21.7 us
    unnamed x54, local copies, waits for them, and re-layouts  13.7 us
  transfers between devices with their start and end apart: 37, of which 18 were waited for; matrix products, arithmetic and copies ran while one was open for 2% of the time, Pallas kernels for 17%

commit v1 on v0

--- a/solution.py
+++ b/solution.py
@@ -231,7 +231,7 @@
 def stack_kernel(*refs):
     out, at = refs[-1], 0
     for ref in refs[:-1]:
-        out[at : at + ref.shape[0], :] = ref[...]
+        out[at : at + ref.shape[0], :] = ref[...].astype(out.dtype)
         at += ref.shape[0]
 
 
@@ -470,7 +470,14 @@
         after=(own_part,),
     )
     wsum = sums[1] + send(sums[0], PARTNER).astype(F32)
-    other = send(wsum[ROWS:], SIBLING)
+    swapped = send(
+        in_vmem(
+            stack_kernel, [jax.ShapeDtypeStruct((128 + ROWS, HALF), F32)],
+            result[128:], wsum[ROWS:],
+        )[0],
+        SIBLING,
+    )
+    other = swapped[128:]
     wgrad = jnp.where(
         core == 0,
         jnp.concatenate([wsum[:ROWS], other], axis=1),
@@ -478,7 +485,7 @@
     )
     new_logits, new_one, new_two = adam(wgrad, weight, probs, logits, moment_one, moment_two)
 
-    other = send(result[128:], SIBLING)
+    other = swapped[:128].astype(BF16)
     output = jnp.where(
         core == 0,
         jnp.concatenate([result[:128], other], axis=1),

time: 178 us -> 189 us (1.062)
  waiting for transfers between devices: 66.9 us -> 79.6 us
  starting transfers between devices: 62.4 us -> 58.4 us
  local copies, waits for them, and re-layouts: 14.6 us -> 16.6 us
    ppermute x37 -> x36, waiting for transfers between devices: 66.9 us -> 79.6 us  [send(): return lax.ppermute(value, AXES, pairs)]
    ppermute x37 -> x36, starting transfers between devices: 62.4 us -> 58.4 us  [send(): return lax.ppermute(value, AXES, pairs)]
    slice x0 -> x2, local copies, waits for them, and re-layouts: none -> 2.36 us  [the longest x1 1.27 us: local(): other = swapped[:128].astype(BF16)]
    pallas_call x17 -> x18, Pallas kernels: 21.7 us -> 21.8 us  [in_vmem(): pl.pallas_call(kernel, in_specs=[IN_VMEM] * len(args), out_specs=[IN_VMEM...]
  transfers between devices with their start and end apart: 37 -> 36, of which waited for: 18 -> 18; matrix products, arithmetic and copies ran while one was open for 2% -> 2% of each run, Pallas kernels for 17% -> 14%
where the time goes in v1:
time: 189 us; the launch traced here: 188 us
  waiting for transfers between devices  79.6 us (42%)
  starting transfers between devices  58.4 us (31%)
  Pallas kernels  30 us (16%)
  local copies, waits for them, and re-layouts  16.6 us (9%)
  other arithmetic  2.71 us (1%)
    ppermute x36, waiting for transfers between devices, send(): return lax.ppermute(value, AXES, pairs)  79.6 us
    ppermute x36, starting transfers between devices, send(): return lax.ppermute(value, AXES, pairs)  58.4 us
    pallas_call x18, Pallas kernels, in_vmem(): pl.pallas_call(kernel, in_specs=[IN_VMEM] * len(args), out_specs=[IN_VMEM...  21.8 us
    unnamed x54, local copies, waits for them, and re-layouts  13.2 us
  transfers between devices with their start and end apart: 36, of which 18 were waited for; matrix products, arithmetic and copies ran while one was open for 2% of the time, Pallas kernels for 14%

profile of v1, /device:TPU:1, one launch (start us, length us, event | category | flops | bytes accessed | tf_op | source)
XLA Modules:
  0.0 188.4 jit_solution(9380526902738518053)
XLA Ops:
  1.7 2.6 %collective-permute-start = (bf16[768,128]{1,0:T(8,128)(2,1)S(1)}, bf16[768,128]{1,0:T(8,128)(2,1)S(1)}, u32[]{:S(2)}, u32[]{:S(2)}) collective-permute-start(bf16[768,128]{1,0:T(8,128)(2,1)S(1)} %bitcast.14), channel_id=1, source_target_pairs={{0,1},{1,0},{2,3},{3,2},{4,5},{5,4},{6,7},{7,6},{8,9},{9,8},{10,11... | collective-permute-start | bytes 589832 | tf_op jit(solution)/shard_map/ppermute | solution.py:70
  4.3 1.3 copy-done
  10.6 6.1 %collective-permute-start.5 = (bf16[96,1536]{1,0:T(8,128)(2,1)S(1)}, bf16[96,1536]{1,0:T(8,128)(2,1)S(1)}, u32[]{:S(2)}, u32[]{:S(2)}) collective-permute-start(bf16[96,1536]{1,0:T(8,128)(2,1)S(1)} %shard_map.219.refs_0_), channel_id=1, source_target_pairs={{0,128},{1,129},{2,130},{3,131},{4,132},{5,133},{6,134},{7,135},{8... | collective-permute-start | bytes 884744 | tf_op jit(solution)/shard_map/ppermute | solution.py:70
  16.7 1.3 collective-permute-start.4
  18.0 2.6 %collective-permute-start.3 = (bf16[96,1536]{1,0:T(8,128)(2,1)S(1)}, bf16[96,1536]{1,0:T(8,128)(2,1)S(1)}, u32[]{:S(2)}, u32[]{:S(2)}) collective-permute-start(bf16[96,1536]{1,0:T(8,128)(2,1)S(1)} %shard_map.219.refs_0_), channel_id=1, source_target_pairs={{0,64},{1,65},{2,66},{3,67},{4,20},{5,21},{6,22},{7,23},{8,72},{9,... | collective-permute-start | bytes 884744 | tf_op jit(solution)/shard_map/ppermute | solution.py:70
  21.7 3.1 %collective-permute-done.5.refs_4_.refs_0_ = bf16[96,1536]{1,0:T(8,128)(2,1)S(1)} collective-permute-done((bf16[96,1536]{1,0:T(8,128)(2,1)S(1)}, bf16[96,1536]{1,0:T(8,128)(2,1)S(1)}, u32[]{:S(2)}, u32[]{:S(2)}) %collective-permute-start.5) | collective-permute-done | bytes 294944 | tf_op jit(solution)/shard_map/ppermute | solution.py:70
  24.8 1.3 collective-permute-start.10
  26.2 2.0 %collective-permute-done.3.refs_2_ = bf16[96,1536]{1,0:T(8,128)(2,1)S(1)} collective-permute-done((bf16[96,1536]{1,0:T(8,128)(2,1)S(1)}, bf16[96,1536]{1,0:T(8,128)(2,1)S(1)}, u32[]{:S(2)}, u32[]{:S(2)}) %collective-permute-start.3) | collective-permute-done | bytes 294944 | tf_op jit(solution)/shard_map/ppermute | solution.py:70
  29.3 1.3 shard_map.221.refs_0_
  30.6 5.9 %collective-permute-start.7 = (bf16[1536,128]{1,0:T(8,128)(2,1)S(1)}, bf16[1536,128]{1,0:T(8,128)(2,1)S(1)}, u32[]{:S(2)}, u32[]{:S(2)}) collective-permute-start(bf16[1536,128]{1,0:T(8,128)(2,1)S(1)} %shard_map.221.refs_0_), channel_id=1, source_target_pairs={{0,2},{1,3},{2,0},{3,1},{4,6},{5,7},{6,4},{7,5},{8,10},{9,11},{10,... | collective-permute-start | bytes 1179656 | tf_op jit(solution)/shard_map/ppermute | solution.py:70
  36.5 1.2 collective-permute-start.13
  37.7 1.5 collective-permute-start.12
  39.2 2.6 %collective-permute-start.9 = (bf16[96,1536]{1,0:T(8,128)(2,1)S(1)}, bf16[96,1536]{1,0:T(8,128)(2,1)S(1)}, u32[]{:S(2)}, u32[]{:S(2)}) collective-permute-start(bf16[96,1536]{1,0:T(8,128)(2,1)S(1)} %collective-permute-done.5.refs_4_.refs_0_), channel_id=1, source_target_pairs={{0,64},{1,65},{2,66},{3,67},{4,20},{5,21},{6,22},{7,23},{8,72},{9,... | collective-permute-start | bytes 884744 | tf_op jit(solution)/shard_map/ppermute | solution.py:70
  42.9 6.8 %collective-permute-done.9.refs_2_ = bf16[96,1536]{1,0:T(8,128)(2,1)S(1)} collective-permute-done((bf16[96,1536]{1,0:T(8,128)(2,1)S(1)}, bf16[96,1536]{1,0:T(8,128)(2,1)S(1)}, u32[]{:S(2)}, u32[]{:S(2)}) %collective-permute-start.9) | collective-permute-done | bytes 294944 | tf_op jit(solution)/shard_map/ppermute | solution.py:70
  49.7 5.4 %collective-permute-done.8.refs_1_ = bf16[96,1536]{1,0:T(8,128)(2,1)S(1)} collective-permute-done((bf16[96,1536]{1,0:T(8,128)(2,1)S(1)}, bf16[96,1536]{1,0:T(8,128)(2,1)S(1)}, u32[]{:S(2)}, u32[]{:S(2)}) %collective-permute-start.8) | collective-permute-done | bytes 294944 | tf_op jit(solution)/shard_map/ppermute | solution.py:70
  55.2 2.7 %collective-permute-start.11 = (bf16[3072,128]{1,0:T(8,128)(2,1)S(1)}, bf16[3072,128]{1,0:T(8,128)(2,1)S(1)}, u32[]{:S(2)}, u32[]{:S(2)}) collective-permute-start(bf16[3072,128]{1,0:T(8,128)(2,1)S(1)} %shard_map.223.mine), channel_id=1, source_target_pairs={{0,4},{1,5},{2,6},{3,7},{4,0},{5,1},{6,2},{7,3},{8,12},{9,13},{10,... | collective-permute-start | bytes 2359304 | tf_op jit(solution)/shard_map/ppermute | solution.py:70
  58.9 1.3 fusion.3
  61.0 2.7 %collective-permute-start.14 = (bf16[384,1536]{1,0:T(8,128)(2,1)S(1)}, bf16[384,1536]{1,0:T(8,128)(2,1)S(1)}, u32[]{:S(2)}, u32[]{:S(2)}) collective-permute-start(bf16[384,1536]{1,0:T(8,128)(2,1)S(1)} %shard_map.222.refs_2_.refs_4_.refs_3_), channel_id=1, source_target_pairs={{0,24},{1,25},{2,26},{3,27},{4,100},{5,101},{6,102},{7,103},{8,0},... | collective-permute-start | bytes 3538952 | tf_op jit(solution)/shard_map/ppermute | solution.py:70
  67.7 2.2 %shard_map.225 = (bf16[384,1536]{1,0:T(8,128)(2,1)S(1)}, bf16[384,1536]{1,0:T(8,128)(2,1)S(1)}) custom-call(bf16[3072,256]{1,0:T(8,128)(2,1)S(1)} %shard_map.224.refs_0_.acts, bf16[256,1536]{1,0:T(8,128)(2,1)S(1)} %pad_maximum_fusion.refs_5_.refs_1_.cot, bf16[384,1536]{1,0:T(8,128)(2,1)} %collective-permute-done.12.refs_2_.refs_3_, ...), custom_call_target="tpu_custom_call" | custom-call | bytes 1 | tf_op jit(solution)/shard_map/pallas_call | solution.py:292
  71.4 4.3 %shard_map.226 = (f32[256,1536]{1,0:T(8,128)S(1)}, f32[1152,128]{1,0:T(8,128)S(1)}, f32[1152,128]{1,0:T(8,128)S(1)}) custom-call(bf16[3072,256]{1,0:T(8,128)(2,1)S(1)} %shard_map.224.refs_0_.acts, bf16[256,1536]{1,0:T(8,128)(2,1)S(1)} %pad_maximum_fusion.refs_5_.refs_1_.cot, bf16[384,1536]{1,0:T(8,128)(2,1)} %shard_map.220.refs_2_, ...), custom_call_target="tpu_custom_call" | custom-call | flops 20000000000 | bytes 1 | tf_op jit(solution)/shard_map/pallas_call | solution.py:292
  75.7 1.9 collective-permute-done.15.refs_3_.refs_5_
  78.2 2.8 %collective-permute-start.18 = (bf16[384,1536]{1,0:T(8,128)(2,1)S(1)}, bf16[384,1536]{1,0:T(8,128)(2,1)S(1)}, u32[]{:S(2)}, u32[]{:S(2)}) collective-permute-start(bf16[384,1536]{1,0:T(8,128)(2,1)S(1)} %get-tuple-element.52), channel_id=1, source_target_pairs={{0,24},{1,25},{2,26},{3,27},{4,100},{5,101},{6,102},{7,103},{8,0},... | collective-permute-start | bytes 3538952 | tf_op jit(solution)/shard_map/ppermute | solution.py:70
  80.9 2.3 %shard_map.228 = (f32[256,1536]{1,0:T(8,128)S(1)}, f32[1152,128]{1,0:T(8,128)S(1)}, f32[1152,128]{1,0:T(8,128)S(1)}) custom-call(bf16[3072,256]{1,0:T(8,128)(2,1)S(1)} %shard_map.224.refs_0_.acts, bf16[256,1536]{1,0:T(8,128)(2,1)S(1)} %pad_maximum_fusion.refs_5_.refs_1_.cot, f32[256,1536]{1,0:T(8,128)S(1)} %get-tuple-element.44.refs_4_.refs_2_, ...), custom_call_target="tpu_custom_call" | custom-call | flops 20000000000 | bytes 1 | tf_op jit(solution)/shard_map/pallas_call | solution.py:292
  83.3 6.7 %collective-permute-done.16.refs_3_ = bf16[384,1536]{1,0:T(8,128)(2,1)S(1)} collective-permute-done((bf16[384,1536]{1,0:T(8,128)(2,1)S(1)}, bf16[384,1536]{1,0:T(8,128)(2,1)S(1)}, u32[]{:S(2)}, u32[]{:S(2)}) %collective-permute-start.16) | collective-permute-done | bytes 1179680 | tf_op jit(solution)/shard_map/ppermute | solution.py:70
  91.0 1.3 collective-permute-start.20
  92.3 1.5 collective-permute-start.23
  95.0 7.6 %collective-permute-done.18.refs_3_ = bf16[384,1536]{1,0:T(8,128)(2,1)S(1)} collective-permute-done((bf16[384,1536]{1,0:T(8,128)(2,1)S(1)}, bf16[384,1536]{1,0:T(8,128)(2,1)S(1)}, u32[]{:S(2)}, u32[]{:S(2)}) %collective-permute-start.18) | collective-permute-done | bytes 1179680 | tf_op jit(solution)/shard_map/ppermute | solution.py:70
  102.9 2.1 %shard_map.232 = (bf16[384,1536]{1,0:T(8,128)(2,1)}, bf16[384,1536]{1,0:T(8,128)(2,1)}) custom-call(bf16[3072,256]{1,0:T(8,128)(2,1)S(1)} %shard_map.224.refs_0_.acts, bf16[256,1536]{1,0:T(8,128)(2,1)S(1)} %pad_maximum_fusion.refs_5_.refs_1_.cot, bf16[384,1536]{1,0:T(8,128)(2,1)S(1)} %collective-permute-done.19.refs_4_.refs_2_, ...), custom_call_target="tpu_custom_call" | custom-call | bytes 1 | tf_op jit(solution)/shard_map/pallas_call | solution.py:292
  105.0 1.2 collective-permute-start.21
  106.2 1.5 collective-permute-start.22
  107.6 1.4 collective-permute-start.30
  109.1 6.4 %collective-permute-done.20.refs_7_.up = bf16[384,1536]{1,0:T(8,128)(2,1)S(1)} collective-permute-done((bf16[384,1536]{1,0:T(8,128)(2,1)S(1)}, bf16[384,1536]{1,0:T(8,128)(2,1)S(1)}, u32[]{:S(2)}, u32[]{:S(2)}) %collective-permute-start.20) | collective-permute-done | bytes 1179680 | tf_op jit(solution)/shard_map/ppermute | solution.py:70
  117.6 1.5 shard_map.233
  119.5 1.9 %shard_map.236 = (f32[1536,128]{1,0:T(8,128)S(1)}, f32[1536,128]{1,0:T(8,128)}) custom-call(s32[128]{0:T(128)S(1)} %pad_add_fusion.place, f32[1536,128]{1,0:T(8,128)S(1)} %get-tuple-element.56.refs_4_.refs_0_, f32[1536,128]{1,0:T(8,128)S(1)} %get-tuple-element.68.refs_1_, f32[1536,128]{1,0:T(8,128)S(1)} %collective-permute-done.30.refs_2_, ...), custom_call_target="tpu_custom_call" | custom-call | bytes 1 | tf_op jit(solution)/shard_map/pallas_call | solution.py:216
  122.3 1.5 collective-permute-start.25
  123.8 6.5 %collective-permute-done.24.one = bf16[96,1536]{1,0:T(8,128)(2,1)S(1)} collective-permute-done((bf16[96,1536]{1,0:T(8,128)(2,1)S(1)}, bf16[96,1536]{1,0:T(8,128)(2,1)S(1)}, u32[]{:S(2)}, u32[]{:S(2)}) %collective-permute-start.24) | collective-permute-done | bytes 294944 | tf_op jit(solution)/shard_map/ppermute | solution.py:70
  131.0 3.7 %collective-permute-done.25.two = bf16[96,1536]{1,0:T(8,128)(2,1)} collective-permute-done((bf16[96,1536]{1,0:T(8,128)(2,1)}, bf16[96,1536]{1,0:T(8,128)(2,1)}, u32[]{:S(2)}, u32[]{:S(2)}) %collective-permute-start.25) | collective-permute-done | bytes 294944 | tf_op jit(solution)/shard_map/ppermute | solution.py:70
  134.7 2.5 %collective-permute-done.26.three = bf16[96,1536]{1,0:T(8,128)(2,1)} collective-permute-done((bf16[96,1536]{1,0:T(8,128)(2,1)}, bf16[96,1536]{1,0:T(8,128)(2,1)}, u32[]{:S(2)}, u32[]{:S(2)}) %collective-permute-start.26) | collective-permute-done | bytes 294944 | tf_op jit(solution)/shard_map/ppermute | solution.py:70
  140.4 4.2 %collective-permute-start.33 = (bf16[96,1536]{1,0:T(8,128)(2,1)S(1)}, bf16[96,1536]{1,0:T(8,128)(2,1)S(1)}, u32[]{:S(2)}, u32[]{:S(2)}) collective-permute-start(bf16[96,1536]{1,0:T(8,128)(2,1)S(1)} %shard_map.234.refs_4_), channel_id=1, source_target_pairs={{0,128},{1,129},{2,130},{3,131},{4,132},{5,133},{6,134},{7,135},{8... | collective-permute-start | bytes 884744 | tf_op jit(solution)/shard_map/ppermute | solution.py:70
  144.7 1.9 %shard_map.235 = (f32[96,1536]{1,0:T(8,128)S(1)}, bf16[96,1536]{1,0:T(8,128)(2,1)S(1)}, bf16[96,1536]{1,0:T(8,128)(2,1)S(1)}, bf16[96,1536]{1,0:T(8,128)(2,1)S(1)}) custom-call(bf16[3072,256]{1,0:T(8,128)(2,1)S(1)} %shard_map.224.refs_0_.acts, bf16[256,1536]{1,0:T(8,128)(2,1)S(1)} %pad_maximum_fusion.refs_5_.refs_1_.cot, ...), custom_call_target="tpu_custom_call" | custom-call | bytes 1 | tf_op jit(solution)/shard_map/pallas_call | solution.py:292
  146.7 2.1 %collective-permute-start.28 = (bf16[96,1536]{1,0:T(8,128)(2,1)S(1)}, bf16[96,1536]{1,0:T(8,128)(2,1)S(1)}, u32[]{:S(2)}, u32[]{:S(2)}) collective-permute-start(bf16[96,1536]{1,0:T(8,128)(2,1)S(1)} %get-tuple-element.66), channel_id=1, source_target_pairs={{0,64},{1,65},{2,66},{3,67},{4,20},{5,21},{6,22},{7,23},{8,72},{9,... | collective-permute-start | bytes 884744 | tf_op jit(solution)/shard_map/ppermute | solution.py:70
  149.4 1.2 shard_map.237
  150.6 6.3 %collective-permute-done.27.refs_1_ = bf16[96,1536]{1,0:T(8,128)(2,1)S(1)} collective-permute-done((bf16[96,1536]{1,0:T(8,128)(2,1)S(1)}, bf16[96,1536]{1,0:T(8,128)(2,1)S(1)}, u32[]{:S(2)}, u32[]{:S(2)}) %collective-permute-start.27) | collective-permute-done | bytes 294944 | tf_op jit(solution)/shard_map/ppermute | solution.py:70
  157.9 2.5 %collective-permute-start.34 = (f32[176,1536]{1,0:T(8,128)S(1)}, f32[176,1536]{1,0:T(8,128)}, u32[]{:S(2)}, u32[]{:S(2)}) collective-permute-start(f32[176,1536]{1,0:T(8,128)S(1)} %shard_map.239), channel_id=1, source_target_pairs={{0,4},{1,5},{2,6},{3,7},{4,0},{5,1},{6,2},{7,3},{8,12},{9,13},{10,... | collective-permute-start | bytes 3244040 | tf_op jit(solution)/shard_map/ppermute | solution.py:70
  160.3 1.5 collective-permute-start.35
  161.8 18.4 %collective-permute-done.35 = f32[768,128]{1,0:T(8,128)S(1)} collective-permute-done((f32[768,128]{1,0:T(8,128)S(1)}, f32[768,128]{1,0:T(8,128)S(1)}, u32[]{:S(2)}, u32[]{:S(2)}) %collective-permute-start.35) | collective-permute-done | bytes 393248 | tf_op jit(solution)/shard_map/ppermute | solution.py:70
  181.1 1.3 slice.34
  185.0 3.4 %shard_map.240 = (f32[6,12,3072]{2,1,0:T(8,128)}, f32[6,12,3072]{2,1,0:T(8,128)}, f32[6,12,3072]{2,1,0:T(8,128)}) custom-call(f32[48,3072]{1,0:T(8,128)S(1)} %maximum_select_fusion.1.wgrad, bf16[48,3072]{1,0:T(8,128)(2,1)S(1)} %copy-done.5, f32[6,12,3072]{2,1,0:T(8,128)S(1)} %copy-done.9, f32[6,12,3072]{2,1,0:T(8,128)S(1)} %copy-done.1, ...), custom_call_target="tpu_custom_call" | custom-call | bytes 1 | tf_op jit(solution)/shard_map/pallas_call | solution.py:156
  (119 shorter events, 32.3 us)
Async XLA Ops:
  1.7 8.9 %collective-permute-start = (bf16[768,128]{1,0:T(8,128)(2,1)S(1)}, bf16[768,128]{1,0:T(8,128)(2,1)S(1)}, u32[]{:S(2)}, u32[]{:S(2)}) collective-permute-start(bf16[768,128]{1,0:T(8,128)(2,1)S(1)} %bitcast.14), channel_id=1, source_target_pairs={{0,1},{1,0},{2,3},{3,2},{4,5},{5,4},{6,7},{7,6},{8,9},{9,8},{10,11... | collective-permute-start | bytes 589832 | tf_op jit(solution)/shard_map/ppermute | solution.py:70
  8.5 2.1 %copy-start.8 = (f32[6,12,3072]{2,1,0:T(8,128)}, f32[6,12,3072]{2,1,0:T(8,128)S(1)}, u32[]{:S(2)}) copy-start(f32[6,12,3072]{2,1,0:T(8,128)S(1)} %get-tuple-element.75.probs) | copy-start | bytes 2654212
  8.6 2.0 %collective-permute-start.1 = (bf16[48,1536]{1,0:T(8,128)(2,1)S(1)}, bf16[48,1536]{1,0:T(8,128)(2,1)S(1)}, u32[]{:S(2)}, u32[]{:S(2)}) collective-permute-start(bf16[48,1536]{1,0:T(8,128)(2,1)S(1)} %get-tuple-element.95), channel_id=1, source_target_pairs={{0,4},{1,5},{2,6},{3,7},{4,0},{5,1},{6,2},{7,3},{8,12},{9,13},{10,... | collective-permute-start | bytes 442376 | tf_op jit(solution)/shard_map/ppermute | solution.py:70
  9.7 16.5 %collective-permute-start.6 = (bf16[128,1536]{1,0:T(8,128)(2,1)S(1)}, bf16[128,1536]{1,0:T(8,128)(2,1)S(1)}, u32[]{:S(2)}, u32[]{:S(2)}) collective-permute-start(bf16[128,1536]{1,0:T(8,128)(2,1)S(1)} %get-tuple-element.92), channel_id=1, source_target_pairs={{0,4},{1,5},{2,6},{3,7},{4,0},{5,1},{6,2},{7,3},{8,12},{9,13},{10,... | collective-permute-start | bytes 1179656 | tf_op jit(solution)/shard_map/ppermute | solution.py:70
  10.6 14.2 %collective-permute-start.5 = (bf16[96,1536]{1,0:T(8,128)(2,1)S(1)}, bf16[96,1536]{1,0:T(8,128)(2,1)S(1)}, u32[]{:S(2)}, u32[]{:S(2)}) collective-permute-start(bf16[96,1536]{1,0:T(8,128)(2,1)S(1)} %shard_map.219.refs_0_), channel_id=1, source_target_pairs={{0,128},{1,129},{2,130},{3,131},{4,132},{5,133},{6,134},{7,135},{8... | collective-permute-start | bytes 884744 | tf_op jit(solution)/shard_map/ppermute | solution.py:70
  16.7 9.4 %collective-permute-start.4 = (bf16[96,1536]{1,0:T(8,128)(2,1)S(1)}, bf16[96,1536]{1,0:T(8,128)(2,1)S(1)}, u32[]{:S(2)}, u32[]{:S(2)}) collective-permute-start(bf16[96,1536]{1,0:T(8,128)(2,1)S(1)} %shard_map.219.refs_0_), channel_id=1, source_target_pairs={{0,32},{1,33},{2,34},{3,35},{4,12},{5,13},{6,14},{7,15},{8,40},{9,... | collective-permute-start | bytes 884744 | tf_op jit(solution)/shard_map/ppermute | solution.py:70
  18.0 10.2 %collective-permute-start.3 = (bf16[96,1536]{1,0:T(8,128)(2,1)S(1)}, bf16[96,1536]{1,0:T(8,128)(2,1)S(1)}, u32[]{:S(2)}, u32[]{:S(2)}) collective-permute-start(bf16[96,1536]{1,0:T(8,128)(2,1)S(1)} %shard_map.219.refs_0_), channel_id=1, source_target_pairs={{0,64},{1,65},{2,66},{3,67},{4,20},{5,21},{6,22},{7,23},{8,72},{9,... | collective-permute-start | bytes 884744 | tf_op jit(solution)/shard_map/ppermute | solution.py:70
  20.6 7.6 %collective-permute-start.2 = (bf16[96,1536]{1,0:T(8,128)(2,1)S(1)}, bf16[96,1536]{1,0:T(8,128)(2,1)S(1)}, u32[]{:S(2)}, u32[]{:S(2)}) collective-permute-start(bf16[96,1536]{1,0:T(8,128)(2,1)S(1)} %shard_map.219.refs_0_), channel_id=1, source_target_pairs={{0,96},{1,97},{2,98},{3,99},{4,28},{5,29},{6,30},{7,31},{8,104},{9... | collective-permute-start | bytes 884744 | tf_op jit(solution)/shard_map/ppermute | solution.py:70
  24.8 17.0 %collective-permute-start.10 = (bf16[96,1536]{1,0:T(8,128)(2,1)S(1)}, bf16[96,1536]{1,0:T(8,128)(2,1)S(1)}, u32[]{:S(2)}, u32[]{:S(2)}) collective-permute-start(bf16[96,1536]{1,0:T(8,128)(2,1)S(1)} %collective-permute-done.5.refs_4_.refs_0_), channel_id=1, source_target_pairs={{0,32},{1,33},{2,34},{3,35},{4,12},{5,13},{6,14},{7,15},{8,40},{9,... | collective-permute-start | bytes 884744 | tf_op jit(solution)/shard_map/ppermute | solution.py:70
  30.6 24.6 %collective-permute-start.7 = (bf16[1536,128]{1,0:T(8,128)(2,1)S(1)}, bf16[1536,128]{1,0:T(8,128)(2,1)S(1)}, u32[]{:S(2)}, u32[]{:S(2)}) collective-permute-start(bf16[1536,128]{1,0:T(8,128)(2,1)S(1)} %shard_map.221.refs_0_), channel_id=1, source_target_pairs={{0,2},{1,3},{2,0},{3,1},{4,6},{5,7},{6,4},{7,5},{8,10},{9,11},{10,... | collective-permute-start | bytes 1179656 | tf_op jit(solution)/shard_map/ppermute | solution.py:70
  36.5 31.2 %collective-permute-start.13 = (bf16[384,1536]{1,0:T(8,128)(2,1)}, bf16[384,1536]{1,0:T(8,128)(2,1)}, u32[]{:S(2)}, u32[]{:S(2)}) collective-permute-start(bf16[384,1536]{1,0:T(8,128)(2,1)} %shard_map.220.refs_2_), channel_id=1, source_target_pairs={{0,8},{1,9},{2,10},{3,11},{4,36},{5,37},{6,38},{7,39},{8,16},{9,17... | collective-permute-start | bytes 3538952 | tf_op jit(solution)/shard_map/ppermute | solution.py:70
  37.7 30.0 %collective-permute-start.12 = (bf16[384,1536]{1,0:T(8,128)(2,1)}, bf16[384,1536]{1,0:T(8,128)(2,1)}, u32[]{:S(2)}, u32[]{:S(2)}) collective-permute-start(bf16[384,1536]{1,0:T(8,128)(2,1)} %shard_map.220.refs_2_), channel_id=1, source_target_pairs={{0,24},{1,25},{2,26},{3,27},{4,100},{5,101},{6,102},{7,103},{8,0},... | collective-permute-start | bytes 3538952 | tf_op jit(solution)/shard_map/ppermute | solution.py:70
  39.2 10.5 %collective-permute-start.9 = (bf16[96,1536]{1,0:T(8,128)(2,1)S(1)}, bf16[96,1536]{1,0:T(8,128)(2,1)S(1)}, u32[]{:S(2)}, u32[]{:S(2)}) collective-permute-start(bf16[96,1536]{1,0:T(8,128)(2,1)S(1)} %collective-permute-done.5.refs_4_.refs_0_), channel_id=1, source_target_pairs={{0,64},{1,65},{2,66},{3,67},{4,20},{5,21},{6,22},{7,23},{8,72},{9,... | collective-permute-start | bytes 884744 | tf_op jit(solution)/shard_map/ppermute | solution.py:70
  41.8 13.3 %collective-permute-start.8 = (bf16[96,1536]{1,0:T(8,128)(2,1)S(1)}, bf16[96,1536]{1,0:T(8,128)(2,1)S(1)}, u32[]{:S(2)}, u32[]{:S(2)}) collective-permute-start(bf16[96,1536]{1,0:T(8,128)(2,1)S(1)} %collective-permute-done.5.refs_4_.refs_0_), channel_id=1, source_target_pairs={{0,96},{1,97},{2,98},{3,99},{4,28},{5,29},{6,30},{7,31},{8,104},{9... | collective-permute-start | bytes 884744 | tf_op jit(solution)/shard_map/ppermute | solution.py:70
  55.1 3.8 %copy-start.22 = (s32[64]{0:T(128)S(1)}, s32[64]{0:T(128)}, u32[]{:S(2)}) copy-start(s32[64]{0:T(128)} %constant.203.clone) | copy-start | bytes 772
  55.2 3.8 %copy-start.23 = (s32[64]{0:T(128)S(1)}, s32[64]{0:T(128)}, u32[]{:S(2)}) copy-start(s32[64]{0:T(128)} %constant.202.clone) | copy-start | bytes 772
  55.2 8.5 %collective-permute-start.11 = (bf16[3072,128]{1,0:T(8,128)(2,1)S(1)}, bf16[3072,128]{1,0:T(8,128)(2,1)S(1)}, u32[]{:S(2)}, u32[]{:S(2)}) collective-permute-start(bf16[3072,128]{1,0:T(8,128)(2,1)S(1)} %shard_map.223.mine), channel_id=1, source_target_pairs={{0,4},{1,5},{2,6},{3,7},{4,0},{5,1},{6,2},{7,3},{8,12},{9,13},{10,... | collective-permute-start | bytes 2359304 | tf_op jit(solution)/shard_map/ppermute | solution.py:70
  61.0 16.6 %collective-permute-start.15 = (bf16[384,1536]{1,0:T(8,128)(2,1)S(1)}, bf16[384,1536]{1,0:T(8,128)(2,1)S(1)}, u32[]{:S(2)}, u32[]{:S(2)}) collective-permute-start(bf16[384,1536]{1,0:T(8,128)(2,1)S(1)} %shard_map.222.refs_2_.refs_4_.refs_3_), channel_id=1, source_target_pairs={{0,8},{1,9},{2,10},{3,11},{4,36},{5,37},{6,38},{7,39},{8,16},{9,17... | collective-permute-start | bytes 3538952 | tf_op jit(solution)/shard_map/ppermute | solution.py:70
  61.0 16.5 %collective-permute-start.14 = (bf16[384,1536]{1,0:T(8,128)(2,1)S(1)}, bf16[384,1536]{1,0:T(8,128)(2,1)S(1)}, u32[]{:S(2)}, u32[]{:S(2)}) collective-permute-start(bf16[384,1536]{1,0:T(8,128)(2,1)S(1)} %shard_map.222.refs_2_.refs_4_.refs_3_), channel_id=1, source_target_pairs={{0,24},{1,25},{2,26},{3,27},{4,100},{5,101},{6,102},{7,103},{8,0},... | collective-permute-start | bytes 3538952 | tf_op jit(solution)/shard_map/ppermute | solution.py:70
  69.9 20.1 %collective-permute-start.16 = (bf16[384,1536]{1,0:T(8,128)(2,1)S(1)}, bf16[384,1536]{1,0:T(8,128)(2,1)S(1)}, u32[]{:S(2)}, u32[]{:S(2)}) collective-permute-start(bf16[384,1536]{1,0:T(8,128)(2,1)S(1)} %get-tuple-element.47), channel_id=1, source_target_pairs={{0,24},{1,25},{2,26},{3,27},{4,100},{5,101},{6,102},{7,103},{8,0},... | collective-permute-start | bytes 3538952 | tf_op jit(solution)/shard_map/ppermute | solution.py:70
  70.6 19.6 %collective-permute-start.17 = (bf16[384,1536]{1,0:T(8,128)(2,1)S(1)}, bf16[384,1536]{1,0:T(8,128)(2,1)S(1)}, u32[]{:S(2)}, u32[]{:S(2)}) collective-permute-start(bf16[384,1536]{1,0:T(8,128)(2,1)S(1)} %get-tuple-element.43.refs_5_), channel_id=1, source_target_pairs={{0,8},{1,9},{2,10},{3,11},{4,36},{5,37},{6,38},{7,39},{8,16},{9,17... | collective-permute-start | bytes 3538952 | tf_op jit(solution)/shard_map/ppermute | solution.py:70
  78.2 24.4 %collective-permute-start.18 = (bf16[384,1536]{1,0:T(8,128)(2,1)S(1)}, bf16[384,1536]{1,0:T(8,128)(2,1)S(1)}, u32[]{:S(2)}, u32[]{:S(2)}) collective-permute-start(bf16[384,1536]{1,0:T(8,128)(2,1)S(1)} %get-tuple-element.52), channel_id=1, source_target_pairs={{0,24},{1,25},{2,26},{3,27},{4,100},{5,101},{6,102},{7,103},{8,0},... | collective-permute-start | bytes 3538952 | tf_op jit(solution)/shard_map/ppermute | solution.py:70
  80.9 21.9 %collective-permute-start.19 = (bf16[384,1536]{1,0:T(8,128)(2,1)S(1)}, bf16[384,1536]{1,0:T(8,128)(2,1)S(1)}, u32[]{:S(2)}, u32[]{:S(2)}) collective-permute-start(bf16[384,1536]{1,0:T(8,128)(2,1)S(1)} %get-tuple-element.45.refs_6_), channel_id=1, source_target_pairs={{0,8},{1,9},{2,10},{3,11},{4,36},{5,37},{6,38},{7,39},{8,16},{9,17... | collective-permute-start | bytes 3538952 | tf_op jit(solution)/shard_map/ppermute | solution.py:70
  91.0 24.5 %collective-permute-start.20 = (bf16[384,1536]{1,0:T(8,128)(2,1)S(1)}, bf16[384,1536]{1,0:T(8,128)(2,1)S(1)}, u32[]{:S(2)}, u32[]{:S(2)}) collective-permute-start(bf16[384,1536]{1,0:T(8,128)(2,1)S(1)} %get-tuple-element.50.refs_7_), channel_id=1, source_target_pairs={{0,8},{1,9},{2,10},{3,11},{4,36},{5,37},{6,38},{7,39},{8,16},{9,17... | collective-permute-start | bytes 3538952 | tf_op jit(solution)/shard_map/ppermute | solution.py:70
  92.3 25.3 %collective-permute-start.23 = (bf16[384,1536]{1,0:T(8,128)(2,1)S(1)}, bf16[384,1536]{1,0:T(8,128)(2,1)S(1)}, u32[]{:S(2)}, u32[]{:S(2)}) collective-permute-start(bf16[384,1536]{1,0:T(8,128)(2,1)S(1)} %get-tuple-element.59), channel_id=1, source_target_pairs={{0,24},{1,25},{2,26},{3,27},{4,100},{5,101},{6,102},{7,103},{8,0},... | collective-permute-start | bytes 3538952 | tf_op jit(solution)/shard_map/ppermute | solution.py:70
  105.0 39.7 %collective-permute-start.21 = (bf16[384,1536]{1,0:T(8,128)(2,1)}, bf16[384,1536]{1,0:T(8,128)(2,1)S(1)}, u32[]{:S(2)}, u32[]{:S(2)}) collective-permute-start(bf16[384,1536]{1,0:T(8,128)(2,1)} %get-tuple-element.57), channel_id=1, source_target_pairs={{0,8},{1,9},{2,10},{3,11},{4,36},{5,37},{6,38},{7,39},{8,16},{9,17... | collective-permute-start | bytes 3538952 | tf_op jit(solution)/shard_map/ppermute | solution.py:70
  106.2 38.5 %collective-permute-start.22 = (bf16[384,1536]{1,0:T(8,128)(2,1)}, bf16[384,1536]{1,0:T(8,128)(2,1)}, u32[]{:S(2)}, u32[]{:S(2)}) collective-permute-start(bf16[384,1536]{1,0:T(8,128)(2,1)} %get-tuple-element.58), channel_id=1, source_target_pairs={{0,24},{1,25},{2,26},{3,27},{4,100},{5,101},{6,102},{7,103},{8,0},... | collective-permute-start | bytes 3538952 | tf_op jit(solution)/shard_map/ppermute | solution.py:70
  107.6 11.5 %collective-permute-start.30 = (f32[1536,128]{1,0:T(8,128)S(1)}, f32[1536,128]{1,0:T(8,128)S(1)}, u32[]{:S(2)}, u32[]{:S(2)}) collective-permute-start(f32[1536,128]{1,0:T(8,128)S(1)} %get-tuple-element.69), channel_id=1, source_target_pairs={{0,4},{1,5},{2,6},{3,7},{4,0},{5,1},{6,2},{7,3},{8,12},{9,13},{10,... | collective-permute-start | bytes 2359304 | tf_op jit(solution)/shard_map/ppermute | solution.py:70
  116.7 2.4 %copy-start.10 = (bf16[256,1536]{1,0:T(8,128)(2,1)}, bf16[256,1536]{1,0:T(8,128)(2,1)S(1)}, u32[]{:S(2)}) copy-start(bf16[256,1536]{1,0:T(8,128)(2,1)S(1)} %get-tuple-element.55) | copy-start | bytes 2359300
  116.7 2.4 %copy-start.24 = (s32[64]{0:T(128)S(1)}, s32[64]{0:T(128)}, u32[]{:S(2)}) copy-start(s32[64]{0:T(128)} %get-tuple-element.97) | copy-start | bytes 772
  116.7 2.4 %copy-start.25 = (s32[64]{0:T(128)S(1)}, s32[64]{0:T(128)}, u32[]{:S(2)}) copy-start(s32[64]{0:T(128)} %get-tuple-element.98) | copy-start | bytes 772
  116.7 2.9 %collective-permute-start.31 = (f32[1536,128]{1,0:T(8,128)S(1)}, f32[1536,128]{1,0:T(8,128)S(1)}, u32[]{:S(2)}, u32[]{:S(2)}) collective-permute-start(f32[1536,128]{1,0:T(8,128)S(1)} %get-tuple-element.70), channel_id=1, source_target_pairs={{0,4},{1,5},{2,6},{3,7},{4,0},{5,1},{6,2},{7,3},{8,12},{9,13},{10,... | collective-permute-start | bytes 2359304 | tf_op jit(solution)/shard_map/ppermute | solution.py:70
  119.1 2.3 %copy-start.16 = (f32[96,1536]{1,0:T(8,128)}, f32[96,1536]{1,0:T(8,128)S(1)}, u32[]{:S(2)}) copy-start(f32[96,1536]{1,0:T(8,128)S(1)} %get-tuple-element.60.own) | copy-start | bytes 1769476
  119.1 11.2 %collective-permute-start.24 = (bf16[96,1536]{1,0:T(8,128)(2,1)S(1)}, bf16[96,1536]{1,0:T(8,128)(2,1)S(1)}, u32[]{:S(2)}, u32[]{:S(2)}) collective-permute-start(bf16[96,1536]{1,0:T(8,128)(2,1)S(1)} %get-tuple-element.61), channel_id=1, source_target_pairs={{0,32},{1,33},{2,34},{3,35},{4,12},{5,13},{6,14},{7,15},{8,40},{9,... | collective-permute-start | bytes 884744 | tf_op jit(solution)/shard_map/ppermute | solution.py:70
  122.3 27.1 %collective-permute-start.32 = (f32[1536,128]{1,0:T(8,128)}, f32[1536,128]{1,0:T(8,128)}, u32[]{:S(2)}, u32[]{:S(2)}) collective-permute-start(f32[1536,128]{1,0:T(8,128)} %get-tuple-element.72), channel_id=1, source_target_pairs={{0,1},{1,0},{2,3},{3,2},{4,5},{5,4},{6,7},{7,6},{8,9},{9,8},{10,11... | collective-permute-start | bytes 2359304 | tf_op jit(solution)/shard_map/ppermute | solution.py:70
  122.3 12.4 %collective-permute-start.25 = (bf16[96,1536]{1,0:T(8,128)(2,1)}, bf16[96,1536]{1,0:T(8,128)(2,1)}, u32[]{:S(2)}, u32[]{:S(2)}) collective-permute-start(bf16[96,1536]{1,0:T(8,128)(2,1)} %get-tuple-element.62), channel_id=1, source_target_pairs={{0,64},{1,65},{2,66},{3,67},{4,20},{5,21},{6,22},{7,23},{8,72},{9,... | collective-permute-start | bytes 884744 | tf_op jit(solution)/shard_map/ppermute | solution.py:70
  131.0 6.2 %collective-permute-start.26 = (bf16[96,1536]{1,0:T(8,128)(2,1)}, bf16[96,1536]{1,0:T(8,128)(2,1)}, u32[]{:S(2)}, u32[]{:S(2)}) collective-permute-start(bf16[96,1536]{1,0:T(8,128)(2,1)} %get-tuple-element.63), channel_id=1, source_target_pairs={{0,96},{1,97},{2,98},{3,99},{4,28},{5,29},{6,30},{7,31},{8,104},{9... | collective-permute-start | bytes 884744 | tf_op jit(solution)/shard_map/ppermute | solution.py:70
  140.4 8.9 %copy-start.11 = (bf16[256,1536]{1,0:T(8,128)(2,1)S(1)}, bf16[256,1536]{1,0:T(8,128)(2,1)}, u32[]{:S(2)}) copy-start(bf16[256,1536]{1,0:T(8,128)(2,1)} %copy-done.10) | copy-start | bytes 2359300
  140.4 17.2 %collective-permute-start.33 = (bf16[96,1536]{1,0:T(8,128)(2,1)S(1)}, bf16[96,1536]{1,0:T(8,128)(2,1)S(1)}, u32[]{:S(2)}, u32[]{:S(2)}) collective-permute-start(bf16[96,1536]{1,0:T(8,128)(2,1)S(1)} %shard_map.234.refs_4_), channel_id=1, source_target_pairs={{0,128},{1,129},{2,130},{3,131},{4,132},{5,133},{6,134},{7,135},{8... | collective-permute-start | bytes 884744 | tf_op jit(solution)/shard_map/ppermute | solution.py:70
  146.6 2.8 %copy-start.13 = (f32[1536,128]{1,0:T(8,128)S(1)}, f32[1536,128]{1,0:T(8,128)}, u32[]{:S(2)}) copy-start(f32[1536,128]{1,0:T(8,128)} %copy-done.12) | copy-start | bytes 2359300
  146.6 10.3 %collective-permute-start.27 = (bf16[96,1536]{1,0:T(8,128)(2,1)S(1)}, bf16[96,1536]{1,0:T(8,128)(2,1)S(1)}, u32[]{:S(2)}, u32[]{:S(2)}) collective-permute-start(bf16[96,1536]{1,0:T(8,128)(2,1)S(1)} %get-tuple-element.65), channel_id=1, source_target_pairs={{0,32},{1,33},{2,34},{3,35},{4,12},{5,13},{6,14},{7,15},{8,40},{9,... | collective-permute-start | bytes 884744 | tf_op jit(solution)/shard_map/ppermute | solution.py:70
  146.7 10.2 %collective-permute-start.28 = (bf16[96,1536]{1,0:T(8,128)(2,1)S(1)}, bf16[96,1536]{1,0:T(8,128)(2,1)S(1)}, u32[]{:S(2)}, u32[]{:S(2)}) collective-permute-start(bf16[96,1536]{1,0:T(8,128)(2,1)S(1)} %get-tuple-element.66), channel_id=1, source_target_pairs={{0,64},{1,65},{2,66},{3,67},{4,20},{5,21},{6,22},{7,23},{8,72},{9,... | collective-permute-start | bytes 884744 | tf_op jit(solution)/shard_map/ppermute | solution.py:70
  148.8 8.8 %collective-permute-start.29 = (bf16[96,1536]{1,0:T(8,128)(2,1)S(1)}, bf16[96,1536]{1,0:T(8,128)(2,1)S(1)}, u32[]{:S(2)}, u32[]{:S(2)}) collective-permute-start(bf16[96,1536]{1,0:T(8,128)(2,1)S(1)} %get-tuple-element.67), channel_id=1, source_target_pairs={{0,96},{1,97},{2,98},{3,99},{4,28},{5,29},{6,30},{7,31},{8,104},{9... | collective-permute-start | bytes 884744 | tf_op jit(solution)/shard_map/ppermute | solution.py:70
  157.9 23.3 %collective-permute-start.34 = (f32[176,1536]{1,0:T(8,128)S(1)}, f32[176,1536]{1,0:T(8,128)}, u32[]{:S(2)}, u32[]{:S(2)}) collective-permute-start(f32[176,1536]{1,0:T(8,128)S(1)} %shard_map.239), channel_id=1, source_target_pairs={{0,4},{1,5},{2,6},{3,7},{4,0},{5,1},{6,2},{7,3},{8,12},{9,13},{10,... | collective-permute-start | bytes 3244040 | tf_op jit(solution)/shard_map/ppermute | solution.py:70
  160.3 19.9 %collective-permute-start.35 = (f32[768,128]{1,0:T(8,128)S(1)}, f32[768,128]{1,0:T(8,128)S(1)}, u32[]{:S(2)}, u32[]{:S(2)}) collective-permute-start(f32[768,128]{1,0:T(8,128)S(1)} %get-tuple-element.74), channel_id=1, source_target_pairs={{0,2},{1,3},{2,0},{3,1},{4,6},{5,7},{6,4},{7,5},{8,10},{9,11},{10,... | collective-permute-start | bytes 1179656 | tf_op jit(solution)/shard_map/ppermute | solution.py:70
  180.2 4.4 %copy-start.9 = (f32[6,12,3072]{2,1,0:T(8,128)S(1)}, f32[6,12,3072]{2,1,0:T(8,128)}, u32[]{:S(2)}) copy-start(f32[6,12,3072]{2,1,0:T(8,128)} %copy-done.8) | copy-start | bytes 2654212
  181.1 3.5 %copy-start.7 = (f32[6,12,3072]{2,1,0:T(8,128)S(1)}, f32[6,12,3072]{2,1,0:T(8,128)}, u32[]{:S(2)}) copy-start(f32[6,12,3072]{2,1,0:T(8,128)} %two.1) | copy-start | bytes 2654212
  182.4 2.3 %copy-start.6 = (f32[6,12,3072]{2,1,0:T(8,128)S(1)}, f32[6,12,3072]{2,1,0:T(8,128)}, u32[]{:S(2)}) copy-start(f32[6,12,3072]{2,1,0:T(8,128)} %one.1) | copy-start | bytes 2654212
  (14 other events, 15.9 us)
